TPU v7x, 512 devices: a whole 4x4x16 slice. The times are simulated.
512 devices in a mesh: section: 4 (over x), row: 8 (over z_hi, core), col: 16 (over y, z_lo).
Axes of the slice: x: 4, y: 4, z: 16 (z_hi: 4, z_lo: 4; z = z_hi * 4 + z_lo), core: 2. Of those that a mesh axis runs over, the one named last changes fastest.
Arguments:
- pair: bfloat16 [256, 256, 128], P(('section', 'row'), 'col'), may hold values from -6 to 6
- labels: int32 [256, 256], P(('section', 'row'), 'col'), may hold values from 0 to 63
- residue_mask: int32 [256], replicated, may hold values 0 or 1
- norm_gain: float32 [128], replicated, may hold values from 0.25 to 1.75
- in_weight: bfloat16 [128, 512], replicated, may hold values from -0.5 to 0.5
- gate_weight: bfloat16 [128, 128], replicated, may hold values from -0.5 to 0.5
- hidden_gain: float32 [128], replicated, may hold values from 0.25 to 1.75
- out_weight: bfloat16 [128, 128], replicated, may hold values from -0.5 to 0.5
- bin_weight: bfloat16 [128, 64], replicated, may hold values from -0.8984375 to 0.8984375
Outputs:
- pair_grad: bfloat16 [256, 256, 128], P(('section', 'row'), 'col')
All inputs are finite; a program needn't handle non-finite values.
Results may differ from a plain program's by a relative error of at most 0.014.
Values may be sent and summed in bfloat16 or wider, within the bound.
A program may use at most 64 MiB of HBM per device.

v0:
```python
import jax
import jax.numpy as jnp
from jax import lax
from jax.sharding import PartitionSpec as P


def partner_2(value, axis, apart):
    mask = 2**apart
    pairs = [(source, source ^ mask) for source in range(lax.axis_size(axis))]
    return lax.ppermute(value, axis, pairs)


def norm_parts(values, gain):
    centre = values - jnp.mean(values, axis=-1, keepdims=True)
    inverse = lax.rsqrt(jnp.mean(centre * centre, axis=-1, keepdims=True) + 1e-05)
    normed = centre * inverse
    return (normed, inverse, normed * gain)


def norm_back(upstream, normed, inverse, gain):
    scaled = upstream * gain
    return inverse * (
        scaled
        - jnp.mean(scaled, axis=-1, keepdims=True)
        - normed * jnp.mean(scaled * normed, axis=-1, keepdims=True)
    )


def mirror(tile):
    tile_rows = tile.shape[0]
    trailing = tile.shape[2:]
    blocks = jnp.moveaxis(tile.reshape((tile_rows, 2, tile_rows) + trailing), 0, 2)
    position = lax.axis_index(("section", "row", "col"))
    low_bits = lax.axis_size("col").bit_length() - 1
    high_bit = position >> low_bits & 1
    own_block = lax.dynamic_index_in_dim(blocks, high_bit, 0, keepdims=False)
    other_block = lax.dynamic_index_in_dim(blocks, 1 - high_bit, 0, keepdims=False)
    arrived = partner_2(other_block, ("section", "row", "col"), low_bits)
    blocks = jnp.where(
        high_bit == 0, jnp.stack([own_block, arrived]), jnp.stack([arrived, own_block])
    )
    for bit_level in range(low_bits):
        carried = blocks
        for bit_number in (bit_level, low_bits + 1 + bit_level):
            carried = partner_2(carried, ("section", "row", "col"), bit_number)
        differ = position >> bit_level & 1 != position >> low_bits + 1 + bit_level & 1
        blocks = jnp.where(differ, carried, blocks)
    return jnp.moveaxis(blocks, 0, 1).reshape(tile.shape)


def fold_cols(values, combine, initial):
    return combine(initial, lax.all_gather(values, "col", axis=1, tiled=True), jnp.int32(0))


def local(
    pair,
    labels,
    residue_mask,
    norm_gain,
    in_weight,
    gate_weight,
    hidden_gain,
    out_weight,
    bin_weight,
):
    tile_rows = pair.shape[0]
    tile_cols = pair.shape[1]
    hidden_width = in_weight.shape[1] // 4
    bin_count = bin_weight.shape[1]
    row_index = lax.axis_index(("section", "row"))
    col_index = lax.axis_index("col")
    mask_rows = lax.dynamic_slice_in_dim(residue_mask, row_index * tile_rows, tile_rows).astype(
        jnp.float32
    )
    mask_cols = lax.dynamic_slice_in_dim(residue_mask, col_index * tile_cols, tile_cols).astype(
        jnp.float32
    )
    pair_mask = (mask_rows[:, None] * mask_cols[None, :])[:, :, None]
    pair_float = pair.astype(jnp.float32)
    normed_in, inverse_in, scaled_in = norm_parts(pair_float, norm_gain)
    inputs = scaled_in.astype(jnp.bfloat16)
    projected = jnp.dot(inputs, in_weight, preferred_element_type=jnp.float32)
    gate_a, value_a, gate_b, value_b = jnp.split(projected, 4, axis=-1)
    sig_a = jax.nn.sigmoid(gate_a)
    sig_b = jax.nn.sigmoid(gate_b)
    left = (sig_a * value_a * pair_mask).astype(jnp.bfloat16)
    right = (sig_b * value_b * pair_mask).astype(jnp.bfloat16)
    rows_left, rows_right = (
        lax.all_gather(left, ("section", "row"), axis=0, tiled=True),
        lax.all_gather(right, ("section", "row"), axis=0, tiled=True),
    )
    empty = jnp.zeros((tile_rows, tile_cols, hidden_width), jnp.float32)
    right_cols = lax.all_gather(mirror(right), ("section", "row"), axis=0, tiled=True)

    def add_block(running, segment, offset):
        return jnp.einsum("ikh,kjh->ijh", segment, right_cols, preferred_element_type=jnp.float32)

    triangle = fold_cols(left, add_block, empty)
    normed_t, inverse_t, scaled_t = norm_parts(triangle, hidden_gain)
    update = jnp.dot(scaled_t.astype(jnp.bfloat16), out_weight, preferred_element_type=jnp.float32)
    gate_out = jax.nn.sigmoid(jnp.dot(inputs, gate_weight, preferred_element_type=jnp.float32))
    pair_out = (pair_float + gate_out * update).astype(jnp.bfloat16)
    logits = jnp.dot(pair_out, bin_weight, preferred_element_type=jnp.float32).astype(jnp.bfloat16)
    symmetric = logits.astype(jnp.float32) + mirror(logits).astype(jnp.float32)
    weights = jnp.exp(symmetric)
    probs = weights / jnp.sum(weights, axis=-1, keepdims=True)
    onehot = (labels[:, :, None] == jnp.arange(bin_count, dtype=jnp.int32)).astype(jnp.float32)
    grad_bins = (pair_mask * (probs - onehot)).astype(jnp.bfloat16)
    grad_sym = (grad_bins.astype(jnp.float32) + mirror(grad_bins).astype(jnp.float32)).astype(
        jnp.bfloat16
    )
    grad_out = jnp.dot(grad_sym, bin_weight.T, preferred_element_type=jnp.float32)
    grad_gate = (grad_out * update * gate_out * (1.0 - gate_out)).astype(jnp.bfloat16)
    grad_update = (grad_out * gate_out).astype(jnp.bfloat16)
    grad_scaled = jnp.dot(grad_update, out_weight.T, preferred_element_type=jnp.float32)
    grad_triangle = norm_back(grad_scaled, normed_t, inverse_t, hidden_gain).astype(jnp.bfloat16)

    def add_left(running, segment, offset):
        return jnp.einsum("ijh,jkh->ikh", segment, rows_right, preferred_element_type=jnp.float32)

    def add_right(running, segment, offset):
        return jnp.einsum("jih,ikh->jkh", segment, rows_left, preferred_element_type=jnp.float32)

    grad_left = fold_cols(grad_triangle, add_left, empty)
    grad_right = fold_cols(mirror(grad_triangle), add_right, empty)
    grad_proj = jnp.concatenate(
        [
            grad_left * value_a * pair_mask * sig_a * (1.0 - sig_a),
            grad_left * sig_a * pair_mask,
            grad_right * value_b * pair_mask * sig_b * (1.0 - sig_b),
            grad_right * sig_b * pair_mask,
        ],
        axis=-1,
    ).astype(jnp.bfloat16)
    grad_inputs = jnp.dot(grad_proj, in_weight.T, preferred_element_type=jnp.float32) + jnp.dot(
        grad_gate, gate_weight.T, preferred_element_type=jnp.float32
    )
    return (grad_out + norm_back(grad_inputs, normed_in, inverse_in, norm_gain)).astype(
        jnp.bfloat16
    )


def solution(mesh):
    placed = (
        P(("section", "row"), "col", None),
        P(("section", "row"), "col"),
        P(),
        P(),
        P(),
        P(),
        P(),
        P(),
        P(),
    )
    return jax.shard_map(
        local,
        mesh=mesh,
        in_specs=placed,
        out_specs=P(("section", "row"), "col", None),
        check_vma=False,
    )
```

profile of v0, /device:TPU:32, one launch (start us, length us, event | category | flops | bytes accessed | tf_op | source)
XLA Modules:
  0.0 555.7 jit_solution(3920876295833236725)
XLA Ops:
  14.3 7.4 %collective-permute-start.1 = (bf16[2,8,8,128]{3,2,0,1:T(8,128)(2,1)S(1)}, bf16[2,8,8,128]{3,2,0,1:T(8,128)(2,1)S(1)}, u32[]{:S(2)}, u32[]{:S(2)}) collective-permute-start(bf16[2,8,8,128]{3,2,0,1:T(8,128)(2,1)S(1)} %maximum_select_fusion), channel_id=1, source_target_pairs={{0,1},{1,0},{2,3},{3,2},{4,5},{5,4},{6,7},{7,6},{8,9},{9,8},{10,11... | collective-permute-start | bytes 98312 | tf_op jit(solution)/shard_map/ppermute | solution.py:10
  23.6 5.6 %collective-permute-start.2 = (bf16[2,8,8,128]{3,2,0,1:T(8,128)(2,1)S(1)}, bf16[2,8,8,128]{3,2,0,1:T(8,128)(2,1)S(1)}, u32[]{:S(2)}, u32[]{:S(2)}) collective-permute-start(bf16[2,8,8,128]{3,2,0,1:T(8,128)(2,1)S(1)} %collective-permute-done.1), channel_id=1, source_target_pairs={{0,32},{1,33},{2,34},{3,35},{4,36},{5,37},{6,38},{7,39},{8,40},{9,... | collective-permute-start | bytes 98312 | tf_op jit(solution)/shard_map/ppermute | solution.py:10
  40.0 11.3 %collective-permute-start.4 = (bf16[2,8,8,128]{3,2,0,1:T(8,128)(2,1)S(1)}, bf16[2,8,8,128]{3,2,0,1:T(8,128)(2,1)S(1)}, u32[]{:S(2)}, u32[]{:S(2)}) collective-permute-start(bf16[2,8,8,128]{3,2,0,1:T(8,128)(2,1)S(1)} %collective-permute-done.3), channel_id=1, source_target_pairs={{0,64},{1,65},{2,66},{3,67},{4,68},{5,69},{6,70},{7,71},{8,72},{9,... | collective-permute-start | bytes 98312 | tf_op jit(solution)/shard_map/ppermute | solution.py:10
  81.8 50.4 %all_gather.19 = bf16[8,256,128]{2,1,0:T(8,128)(2,1)S(1)} all-gather(bf16[8,16,128]{2,1,0:T(8,128)(2,1)S(1)} %get-tuple-element.15), channel_id=1, replica_groups=mesh['section'=4,'row'=8,'col'=16] {'col'}, dimensions={1}, use_global_device_ids=true | all-gather | bytes 557056 | tf_op jit(solution)/shard_map/all_gather | solution.py:52
  133.6 81.4 %all-gather.4.cloned.1.call-done = bf16[256,16,128]{1,0,2:T(8,128)(2,1)} async-done(((bf16[8,16,128]{1,0,2:T(8,128)(2,1)}), bf16[256,16,128]{1,0,2:T(8,128)(2,1)}) %all-gather.4.cloned.1.call-update) | async-done | bytes 1048592 | tf_op jit(solution)/shard_map/all_gather | solution.py:93
  214.9 4.6 fusion.76
  223.5 18.0 %collective-permute-start.10 = (bf16[2,8,8,64]{3,1,2,0:T(8,128)(2,1)S(1)}, bf16[2,8,8,64]{3,1,2,0:T(8,128)(2,1)S(1)}, u32[]{:S(2)}, u32[]{:S(2)}) collective-permute-start(bf16[2,8,8,64]{3,1,2,0:T(8,128)(2,1)S(1)} %maximum_select_fusion.1), channel_id=1, source_target_pairs={{0,1},{1,0},{2,3},{3,2},{4,5},{5,4},{6,7},{7,6},{8,9},{9,8},{10,11... | collective-permute-start | bytes 49160 | tf_op jit(solution)/shard_map/ppermute | solution.py:10
  243.4 5.0 collective-permute-start.11
  248.4 5.1 collective-permute-done.11
  260.2 4.5 collective-permute-start.13
  264.8 10.1 %collective-permute-done.13 = bf16[2,8,8,64]{3,1,2,0:T(8,128)(2,1)S(1)} collective-permute-done((bf16[2,8,8,64]{3,1,2,0:T(8,128)(2,1)S(1)}, bf16[2,8,8,64]{3,1,2,0:T(8,128)(2,1)S(1)}, u32[]{:S(2)}, u32[]{:S(2)}) %collective-permute-start.13) | collective-permute-done | bytes 16416 | tf_op jit(solution)/shard_map/ppermute | solution.py:10
  286.6 4.7 collective-permute-start.16
  293.9 4.6 collective-permute-start.17
  310.4 4.9 collective-permute-start.20
  315.4 6.5 %collective-permute-done.20 = bf16[2,8,8,64]{3,1,2,0:T(8,128)(2,1)S(1)} collective-permute-done((bf16[2,8,8,64]{3,1,2,0:T(8,128)(2,1)S(1)}, bf16[2,8,8,64]{3,1,2,0:T(8,128)(2,1)S(1)}, u32[]{:S(2)}, u32[]{:S(2)}) %collective-permute-start.20) | collective-permute-done | bytes 16416 | tf_op jit(solution)/shard_map/ppermute | solution.py:10
  323.9 4.8 collective-permute-done.21
  328.6 4.7 collective-permute-start.22
  333.3 9.8 %collective-permute-done.22 = bf16[2,8,8,64]{3,1,2,0:T(8,128)(2,1)S(1)} collective-permute-done((bf16[2,8,8,64]{3,1,2,0:T(8,128)(2,1)S(1)}, bf16[2,8,8,64]{3,1,2,0:T(8,128)(2,1)S(1)}, u32[]{:S(2)}, u32[]{:S(2)}) %collective-permute-start.22) | collective-permute-done | bytes 16416 | tf_op jit(solution)/shard_map/ppermute | solution.py:10
  354.8 5.1 collective-permute-start.25
  362.1 4.9 collective-permute-start.26
  373.1 5.3 collective-permute-start.28
  383.2 7.1 %collective-permute-done.29 = bf16[2,8,8,128]{3,2,0,1:T(8,128)(2,1)S(1)} collective-permute-done((bf16[2,8,8,128]{3,2,0,1:T(8,128)(2,1)S(1)}, bf16[2,8,8,128]{3,2,0,1:T(8,128)(2,1)S(1)}, u32[]{:S(2)}, u32[]{:S(2)}) %collective-permute-start.29) | collective-permute-done | bytes 32800 | tf_op jit(solution)/shard_map/ppermute | solution.py:10
  392.2 5.1 collective-permute-done.30
  397.2 5.5 collective-permute-start.31
  402.7 9.4 %collective-permute-done.31 = bf16[2,8,8,128]{3,2,0,1:T(8,128)(2,1)S(1)} collective-permute-done((bf16[2,8,8,128]{3,2,0,1:T(8,128)(2,1)S(1)}, bf16[2,8,8,128]{3,2,0,1:T(8,128)(2,1)S(1)}, u32[]{:S(2)}, u32[]{:S(2)}) %collective-permute-start.31) | collective-permute-done | bytes 32800 | tf_op jit(solution)/shard_map/ppermute | solution.py:10
  421.0 7.6 %copy.79 = bf16[256,16,128]{1,0,2:T(8,128)(2,1)} copy(bf16[256,16,128]{2,1,0:T(8,128)(2,1)} %all-gather.6.cloned.1.call-done) | data formatting | bytes 2097152 | tf_op jit(solution)/shard_map/all_gather | solution.py:90
  432.8 7.4 %copy.85 = bf16[256,16,128]{1,0,2:T(8,128)(2,1)} copy(bf16[256,16,128]{2,1,0:T(8,128)(2,1)} %all-gather.8.cloned.1.call-done) | data formatting | bytes 2097152 | tf_op jit(solution)/shard_map/all_gather | solution.py:89
  440.3 4.9 collective-permute-start.34
  445.2 43.7 %all_gather.21 = bf16[8,256,128]{2,0,1:T(8,128)(2,1)S(1)} all-gather(bf16[8,16,128]{2,0,1:T(8,128)(2,1)S(1)} %copy.78), channel_id=1, replica_groups=mesh['section'=4,'row'=8,'col'=16] {'col'}, dimensions={1}, use_global_device_ids=true | all-gather | bytes 557056 | tf_op jit(solution)/shard_map/all_gather | solution.py:52
  492.9 4.6 fusion.77
  497.7 44.7 %all_gather.23 = bf16[8,256,128]{2,0,1:T(8,128)(2,1)S(1)} all-gather(bf16[8,16,128]{2,0,1:T(8,128)(2,1)S(1)} %copy.84), channel_id=1, replica_groups=mesh['section'=4,'row'=8,'col'=16] {'col'}, dimensions={1}, use_global_device_ids=true | all-gather | bytes 557056 | tf_op jit(solution)/shard_map/all_gather | solution.py:52
  543.1 4.6 fusion.78
  (141 shorter events, 138.6 us)
Async XLA Ops:
  6.6 208.4 %all-gather.4.cloned.1.call-start = ((), (), s32[]{:S(2)}) async-start(), calls=%async_computation | async-start | bytes 8650752 | tf_op jit(solution)/shard_map/all_gather | solution.py:93
  14.3 9.3 %collective-permute-start.1 = (bf16[2,8,8,128]{3,2,0,1:T(8,128)(2,1)S(1)}, bf16[2,8,8,128]{3,2,0,1:T(8,128)(2,1)S(1)}, u32[]{:S(2)}, u32[]{:S(2)}) collective-permute-start(bf16[2,8,8,128]{3,2,0,1:T(8,128)(2,1)S(1)} %maximum_select_fusion), channel_id=1, source_target_pairs={{0,1},{1,0},{2,3},{3,2},{4,5},{5,4},{6,7},{7,6},{8,9},{9,8},{10,11... | collective-permute-start | bytes 98312 | tf_op jit(solution)/shard_map/ppermute | solution.py:10
  23.6 9.7 %collective-permute-start.2 = (bf16[2,8,8,128]{3,2,0,1:T(8,128)(2,1)S(1)}, bf16[2,8,8,128]{3,2,0,1:T(8,128)(2,1)S(1)}, u32[]{:S(2)}, u32[]{:S(2)}) collective-permute-start(bf16[2,8,8,128]{3,2,0,1:T(8,128)(2,1)S(1)} %collective-permute-done.1), channel_id=1, source_target_pairs={{0,32},{1,33},{2,34},{3,35},{4,36},{5,37},{6,38},{7,39},{8,40},{9,... | collective-permute-start | bytes 98312 | tf_op jit(solution)/shard_map/ppermute | solution.py:10
  33.3 6.7 %collective-permute-start.3 = (bf16[2,8,8,128]{3,2,0,1:T(8,128)(2,1)S(1)}, bf16[2,8,8,128]{3,2,0,1:T(8,128)(2,1)S(1)}, u32[]{:S(2)}, u32[]{:S(2)}) collective-permute-start(bf16[2,8,8,128]{3,2,0,1:T(8,128)(2,1)S(1)} %broadcast_select_fusion.7), channel_id=1, source_target_pairs={{0,2},{1,3},{2,0},{3,1},{4,6},{5,7},{6,4},{7,5},{8,10},{9,11},{10,... | collective-permute-start | bytes 98312 | tf_op jit(solution)/shard_map/ppermute | solution.py:10
  40.0 14.5 %collective-permute-start.4 = (bf16[2,8,8,128]{3,2,0,1:T(8,128)(2,1)S(1)}, bf16[2,8,8,128]{3,2,0,1:T(8,128)(2,1)S(1)}, u32[]{:S(2)}, u32[]{:S(2)}) collective-permute-start(bf16[2,8,8,128]{3,2,0,1:T(8,128)(2,1)S(1)} %collective-permute-done.3), channel_id=1, source_target_pairs={{0,64},{1,65},{2,66},{3,67},{4,68},{5,69},{6,70},{7,71},{8,72},{9,... | collective-permute-start | bytes 98312 | tf_op jit(solution)/shard_map/ppermute | solution.py:10
  54.5 5.8 %collective-permute-start.5 = (bf16[2,8,8,128]{3,2,0,1:T(8,128)(2,1)S(1)}, bf16[2,8,8,128]{3,2,0,1:T(8,128)(2,1)S(1)}, u32[]{:S(2)}, u32[]{:S(2)}) collective-permute-start(bf16[2,8,8,128]{3,2,0,1:T(8,128)(2,1)S(1)} %broadcast_select_fusion.9), channel_id=1, source_target_pairs={{0,4},{1,5},{2,6},{3,7},{4,0},{5,1},{6,2},{7,3},{8,12},{9,13},{10,... | collective-permute-start | bytes 98312 | tf_op jit(solution)/shard_map/ppermute | solution.py:10
  66.2 7.3 %collective-permute-start.7 = (bf16[2,8,8,128]{3,2,0,1:T(8,128)(2,1)S(1)}, bf16[2,8,8,128]{3,2,0,1:T(8,128)(2,1)S(1)}, u32[]{:S(2)}, u32[]{:S(2)}) collective-permute-start(bf16[2,8,8,128]{3,2,0,1:T(8,128)(2,1)S(1)} %broadcast_select_fusion.11), channel_id=1, source_target_pairs={{0,8},{1,9},{2,10},{3,11},{4,12},{5,13},{6,14},{7,15},{8,0},{9,1},... | collective-permute-start | bytes 98312 | tf_op jit(solution)/shard_map/ppermute | solution.py:10
  73.5 7.3 %collective-permute-start.8 = (bf16[2,8,8,128]{3,2,0,1:T(8,128)(2,1)S(1)}, bf16[2,8,8,128]{3,2,0,1:T(8,128)(2,1)S(1)}, u32[]{:S(2)}, u32[]{:S(2)}) collective-permute-start(bf16[2,8,8,128]{3,2,0,1:T(8,128)(2,1)S(1)} %collective-permute-done.7), channel_id=1, source_target_pairs={{0,256},{1,257},{2,258},{3,259},{4,260},{5,261},{6,262},{7,263},{8... | collective-permute-start | bytes 98312 | tf_op jit(solution)/shard_map/ppermute | solution.py:10
  81.7 339.3 %all-gather.6.cloned.1.call-start = ((), (), s32[]{:S(2)}) async-start(), calls=%async_computation.1 | async-start | bytes 1081344 | tf_op jit(solution)/shard_map/all_gather | solution.py:90
  223.5 19.9 %collective-permute-start.10 = (bf16[2,8,8,64]{3,1,2,0:T(8,128)(2,1)S(1)}, bf16[2,8,8,64]{3,1,2,0:T(8,128)(2,1)S(1)}, u32[]{:S(2)}, u32[]{:S(2)}) collective-permute-start(bf16[2,8,8,64]{3,1,2,0:T(8,128)(2,1)S(1)} %maximum_select_fusion.1), channel_id=1, source_target_pairs={{0,1},{1,0},{2,3},{3,2},{4,5},{5,4},{6,7},{7,6},{8,9},{9,8},{10,11... | collective-permute-start | bytes 49160 | tf_op jit(solution)/shard_map/ppermute | solution.py:10
  243.4 10.1 %collective-permute-start.11 = (bf16[2,8,8,64]{3,1,2,0:T(8,128)(2,1)S(1)}, bf16[2,8,8,64]{3,1,2,0:T(8,128)(2,1)S(1)}, u32[]{:S(2)}, u32[]{:S(2)}) collective-permute-start(bf16[2,8,8,64]{3,1,2,0:T(8,128)(2,1)S(1)} %collective-permute-done.10), channel_id=1, source_target_pairs={{0,32},{1,33},{2,34},{3,35},{4,36},{5,37},{6,38},{7,39},{8,40},{9,... | collective-permute-start | bytes 49160 | tf_op jit(solution)/shard_map/ppermute | solution.py:10
  253.5 6.7 %collective-permute-start.12 = (bf16[2,8,8,64]{3,1,2,0:T(8,128)(2,1)S(1)}, bf16[2,8,8,64]{3,1,2,0:T(8,128)(2,1)S(1)}, u32[]{:S(2)}, u32[]{:S(2)}) collective-permute-start(bf16[2,8,8,64]{3,1,2,0:T(8,128)(2,1)S(1)} %broadcast_select_fusion.1), channel_id=1, source_target_pairs={{0,2},{1,3},{2,0},{3,1},{4,6},{5,7},{6,4},{7,5},{8,10},{9,11},{10,... | collective-permute-start | bytes 49160 | tf_op jit(solution)/shard_map/ppermute | solution.py:10
  260.2 14.8 %collective-permute-start.13 = (bf16[2,8,8,64]{3,1,2,0:T(8,128)(2,1)S(1)}, bf16[2,8,8,64]{3,1,2,0:T(8,128)(2,1)S(1)}, u32[]{:S(2)}, u32[]{:S(2)}) collective-permute-start(bf16[2,8,8,64]{3,1,2,0:T(8,128)(2,1)S(1)} %collective-permute-done.12), channel_id=1, source_target_pairs={{0,64},{1,65},{2,66},{3,67},{4,68},{5,69},{6,70},{7,71},{8,72},{9,... | collective-permute-start | bytes 49160 | tf_op jit(solution)/shard_map/ppermute | solution.py:10
  264.8 168.0 %all-gather.8.cloned.1.call-start = ((), (), s32[]{:S(2)}) async-start(), calls=%async_computation.2 | async-start | bytes 1081344 | tf_op jit(solution)/shard_map/all_gather | solution.py:89
  275.0 5.8 %collective-permute-start.14 = (bf16[2,8,8,64]{3,1,2,0:T(8,128)(2,1)S(1)}, bf16[2,8,8,64]{3,1,2,0:T(8,128)(2,1)S(1)}, u32[]{:S(2)}, u32[]{:S(2)}) collective-permute-start(bf16[2,8,8,64]{3,1,2,0:T(8,128)(2,1)S(1)} %broadcast_select_fusion.3), channel_id=1, source_target_pairs={{0,4},{1,5},{2,6},{3,7},{4,0},{5,1},{6,2},{7,3},{8,12},{9,13},{10,... | collective-permute-start | bytes 49160 | tf_op jit(solution)/shard_map/ppermute | solution.py:10
  286.6 7.3 %collective-permute-start.16 = (bf16[2,8,8,64]{3,1,2,0:T(8,128)(2,1)S(1)}, bf16[2,8,8,64]{3,1,2,0:T(8,128)(2,1)S(1)}, u32[]{:S(2)}, u32[]{:S(2)}) collective-permute-start(bf16[2,8,8,64]{3,1,2,0:T(8,128)(2,1)S(1)} %broadcast_select_fusion.5), channel_id=1, source_target_pairs={{0,8},{1,9},{2,10},{3,11},{4,12},{5,13},{6,14},{7,15},{8,0},{9,1},... | collective-permute-start | bytes 49160 | tf_op jit(solution)/shard_map/ppermute | solution.py:10
  293.9 7.3 %collective-permute-start.17 = (bf16[2,8,8,64]{3,1,2,0:T(8,128)(2,1)S(1)}, bf16[2,8,8,64]{3,1,2,0:T(8,128)(2,1)S(1)}, u32[]{:S(2)}, u32[]{:S(2)}) collective-permute-start(bf16[2,8,8,64]{3,1,2,0:T(8,128)(2,1)S(1)} %collective-permute-done.16), channel_id=1, source_target_pairs={{0,256},{1,257},{2,258},{3,259},{4,260},{5,261},{6,262},{7,263},{8... | collective-permute-start | bytes 49160 | tf_op jit(solution)/shard_map/ppermute | solution.py:10
  304.6 5.8 %collective-permute-start.19 = (bf16[2,8,8,64]{3,1,2,0:T(8,128)(2,1)S(1)}, bf16[2,8,8,64]{3,1,2,0:T(8,128)(2,1)S(1)}, u32[]{:S(2)}, u32[]{:S(2)}) collective-permute-start(bf16[2,8,8,64]{3,1,2,0:T(8,128)(2,1)S(1)} %maximum_select_fusion.2), channel_id=1, source_target_pairs={{0,1},{1,0},{2,3},{3,2},{4,5},{5,4},{6,7},{7,6},{8,9},{9,8},{10,11... | collective-permute-start | bytes 49160 | tf_op jit(solution)/shard_map/ppermute | solution.py:10
  310.4 11.5 %collective-permute-start.20 = (bf16[2,8,8,64]{3,1,2,0:T(8,128)(2,1)S(1)}, bf16[2,8,8,64]{3,1,2,0:T(8,128)(2,1)S(1)}, u32[]{:S(2)}, u32[]{:S(2)}) collective-permute-start(bf16[2,8,8,64]{3,1,2,0:T(8,128)(2,1)S(1)} %collective-permute-done.19), channel_id=1, source_target_pairs={{0,32},{1,33},{2,34},{3,35},{4,36},{5,37},{6,38},{7,39},{8,40},{9,... | collective-permute-start | bytes 49160 | tf_op jit(solution)/shard_map/ppermute | solution.py:10
  321.9 6.7 %collective-permute-start.21 = (bf16[2,8,8,64]{3,1,2,0:T(8,128)(2,1)S(1)}, bf16[2,8,8,64]{3,1,2,0:T(8,128)(2,1)S(1)}, u32[]{:S(2)}, u32[]{:S(2)}) collective-permute-start(bf16[2,8,8,64]{3,1,2,0:T(8,128)(2,1)S(1)} %broadcast_select_fusion), channel_id=1, source_target_pairs={{0,2},{1,3},{2,0},{3,1},{4,6},{5,7},{6,4},{7,5},{8,10},{9,11},{10,... | collective-permute-start | bytes 49160 | tf_op jit(solution)/shard_map/ppermute | solution.py:10
  328.6 14.5 %collective-permute-start.22 = (bf16[2,8,8,64]{3,1,2,0:T(8,128)(2,1)S(1)}, bf16[2,8,8,64]{3,1,2,0:T(8,128)(2,1)S(1)}, u32[]{:S(2)}, u32[]{:S(2)}) collective-permute-start(bf16[2,8,8,64]{3,1,2,0:T(8,128)(2,1)S(1)} %collective-permute-done.21), channel_id=1, source_target_pairs={{0,64},{1,65},{2,66},{3,67},{4,68},{5,69},{6,70},{7,71},{8,72},{9,... | collective-permute-start | bytes 49160 | tf_op jit(solution)/shard_map/ppermute | solution.py:10
  343.2 5.8 %collective-permute-start.23 = (bf16[2,8,8,64]{3,1,2,0:T(8,128)(2,1)S(1)}, bf16[2,8,8,64]{3,1,2,0:T(8,128)(2,1)S(1)}, u32[]{:S(2)}, u32[]{:S(2)}) collective-permute-start(bf16[2,8,8,64]{3,1,2,0:T(8,128)(2,1)S(1)} %broadcast_select_fusion.2), channel_id=1, source_target_pairs={{0,4},{1,5},{2,6},{3,7},{4,0},{5,1},{6,2},{7,3},{8,12},{9,13},{10,... | collective-permute-start | bytes 49160 | tf_op jit(solution)/shard_map/ppermute | solution.py:10
  354.8 7.3 %collective-permute-start.25 = (bf16[2,8,8,64]{3,1,2,0:T(8,128)(2,1)S(1)}, bf16[2,8,8,64]{3,1,2,0:T(8,128)(2,1)S(1)}, u32[]{:S(2)}, u32[]{:S(2)}) collective-permute-start(bf16[2,8,8,64]{3,1,2,0:T(8,128)(2,1)S(1)} %broadcast_select_fusion.4), channel_id=1, source_target_pairs={{0,8},{1,9},{2,10},{3,11},{4,12},{5,13},{6,14},{7,15},{8,0},{9,1},... | collective-permute-start | bytes 49160 | tf_op jit(solution)/shard_map/ppermute | solution.py:10
  362.1 7.3 %collective-permute-start.26 = (bf16[2,8,8,64]{3,1,2,0:T(8,128)(2,1)S(1)}, bf16[2,8,8,64]{3,1,2,0:T(8,128)(2,1)S(1)}, u32[]{:S(2)}, u32[]{:S(2)}) collective-permute-start(bf16[2,8,8,64]{3,1,2,0:T(8,128)(2,1)S(1)} %collective-permute-done.25), channel_id=1, source_target_pairs={{0,256},{1,257},{2,258},{3,259},{4,260},{5,261},{6,262},{7,263},{8... | collective-permute-start | bytes 49160 | tf_op jit(solution)/shard_map/ppermute | solution.py:10
  373.1 7.1 %collective-permute-start.28 = (bf16[2,8,8,128]{3,2,0,1:T(8,128)(2,1)S(1)}, bf16[2,8,8,128]{3,2,0,1:T(8,128)(2,1)S(1)}, u32[]{:S(2)}, u32[]{:S(2)}) collective-permute-start(bf16[2,8,8,128]{3,2,0,1:T(8,128)(2,1)S(1)} %maximum_select_fusion.3), channel_id=1, source_target_pairs={{0,1},{1,0},{2,3},{3,2},{4,5},{5,4},{6,7},{7,6},{8,9},{9,8},{10,11... | collective-permute-start | bytes 98312 | tf_op jit(solution)/shard_map/ppermute | solution.py:10
  380.2 10.0 %collective-permute-start.29 = (bf16[2,8,8,128]{3,2,0,1:T(8,128)(2,1)S(1)}, bf16[2,8,8,128]{3,2,0,1:T(8,128)(2,1)S(1)}, u32[]{:S(2)}, u32[]{:S(2)}) collective-permute-start(bf16[2,8,8,128]{3,2,0,1:T(8,128)(2,1)S(1)} %collective-permute-done.28), channel_id=1, source_target_pairs={{0,32},{1,33},{2,34},{3,35},{4,36},{5,37},{6,38},{7,39},{8,40},{9,... | collective-permute-start | bytes 98312 | tf_op jit(solution)/shard_map/ppermute | solution.py:10
  390.2 7.0 %collective-permute-start.30 = (bf16[2,8,8,128]{3,2,0,1:T(8,128)(2,1)S(1)}, bf16[2,8,8,128]{3,2,0,1:T(8,128)(2,1)S(1)}, u32[]{:S(2)}, u32[]{:S(2)}) collective-permute-start(bf16[2,8,8,128]{3,2,0,1:T(8,128)(2,1)S(1)} %broadcast_select_fusion.6), channel_id=1, source_target_pairs={{0,2},{1,3},{2,0},{3,1},{4,6},{5,7},{6,4},{7,5},{8,10},{9,11},{10,... | collective-permute-start | bytes 98312 | tf_op jit(solution)/shard_map/ppermute | solution.py:10
  397.2 14.9 %collective-permute-start.31 = (bf16[2,8,8,128]{3,2,0,1:T(8,128)(2,1)S(1)}, bf16[2,8,8,128]{3,2,0,1:T(8,128)(2,1)S(1)}, u32[]{:S(2)}, u32[]{:S(2)}) collective-permute-start(bf16[2,8,8,128]{3,2,0,1:T(8,128)(2,1)S(1)} %collective-permute-done.30), channel_id=1, source_target_pairs={{0,64},{1,65},{2,66},{3,67},{4,68},{5,69},{6,70},{7,71},{8,72},{9,... | collective-permute-start | bytes 98312 | tf_op jit(solution)/shard_map/ppermute | solution.py:10
  412.1 5.8 %collective-permute-start.32 = (bf16[2,8,8,128]{3,2,0,1:T(8,128)(2,1)S(1)}, bf16[2,8,8,128]{3,2,0,1:T(8,128)(2,1)S(1)}, u32[]{:S(2)}, u32[]{:S(2)}) collective-permute-start(bf16[2,8,8,128]{3,2,0,1:T(8,128)(2,1)S(1)} %broadcast_select_fusion.8), channel_id=1, source_target_pairs={{0,4},{1,5},{2,6},{3,7},{4,0},{5,1},{6,2},{7,3},{8,12},{9,13},{10,... | collective-permute-start | bytes 98312 | tf_op jit(solution)/shard_map/ppermute | solution.py:10
  417.9 22.3 %collective-permute-start.33 = (bf16[2,8,8,128]{3,2,0,1:T(8,128)(2,1)S(1)}, bf16[2,8,8,128]{3,2,0,1:T(8,128)(2,1)S(1)}, u32[]{:S(2)}, u32[]{:S(2)}) collective-permute-start(bf16[2,8,8,128]{3,2,0,1:T(8,128)(2,1)S(1)} %collective-permute-done.32), channel_id=1, source_target_pairs={{0,128},{1,129},{2,130},{3,131},{4,132},{5,133},{6,134},{7,135},{8... | collective-permute-start | bytes 98312 | tf_op jit(solution)/shard_map/ppermute | solution.py:10
  440.3 49.2 %collective-permute-start.34 = (bf16[2,8,8,128]{3,2,0,1:T(8,128)(2,1)S(1)}, bf16[2,8,8,128]{3,2,0,1:T(8,128)(2,1)S(1)}, u32[]{:S(2)}, u32[]{:S(2)}) collective-permute-start(bf16[2,8,8,128]{3,2,0,1:T(8,128)(2,1)S(1)} %broadcast_select_fusion.10), channel_id=1, source_target_pairs={{0,8},{1,9},{2,10},{3,11},{4,12},{5,13},{6,14},{7,15},{8,0},{9,1},... | collective-permute-start | bytes 98312 | tf_op jit(solution)/shard_map/ppermute | solution.py:10
  489.5 8.2 %collective-permute-start.35 = (bf16[2,8,8,128]{3,2,0,1:T(8,128)(2,1)S(1)}, bf16[2,8,8,128]{3,2,0,1:T(8,128)(2,1)S(1)}, u32[]{:S(2)}, u32[]{:S(2)}) collective-permute-start(bf16[2,8,8,128]{3,2,0,1:T(8,128)(2,1)S(1)} %collective-permute-done.34), channel_id=1, source_target_pairs={{0,256},{1,257},{2,258},{3,259},{4,260},{5,261},{6,262},{7,263},{8... | collective-permute-start | bytes 98312 | tf_op jit(solution)/shard_map/ppermute | solution.py:10
  (17 other events, 1893.0 us)
Sparse Core Ops, SparseCore 0:
  81.8 133.0 all-gather.3
  264.9 69.2 all-gather.5
  367.2 65.5 all-gather.7
where the time goes:
time: 558 us; the launch traced here: 556 us
  waiting for transfers between devices  208 us (37%)
  starting transfers between devices  154 us (28%)
  blocking collectives  139 us (25%)
  local copies, waits for them, and re-layouts  18.2 us (3%)
  matrix products  16.9 us (3%)
  between operations  13.9 us (2%)
    ppermute x36, starting transfers between devices, partner_2(): return lax.ppermute(value, axis, pairs)  154 us
    all_gather x3, blocking collectives, fold_cols(): lax.all_gather(values, 'col', axis=1, tiled=True)  139 us
    ppermute x36, waiting for transfers between devices, partner_2(): return lax.ppermute(value, axis, pairs)  123 us
    all_gather x1, waiting for transfers between devices, local(): lax.all_gather(mirror(right), ('section', 'row'), axis=0, tiled=True)  81.4 us
  transfers between devices with their start and end apart: 39, of which 35 were waited for; matrix products, arithmetic and copies ran while one was open for 4% of the time, Pallas kernels for 0%

commit v1 on v0

v1 whole, which is shorter than its diff:
```python
import functools

import jax
import jax.numpy as jnp
from jax import lax
from jax.experimental import pallas as pl
from jax.experimental.pallas import tpu as pltpu
from jax.sharding import PartitionSpec as P

MESH = pl.DeviceIdType.MESH
F32 = jnp.float32
BF16 = jnp.bfloat16


def norm_parts(values, gain):
    centre = values - jnp.mean(values, axis=-1, keepdims=True)
    inverse = lax.rsqrt(jnp.mean(centre * centre, axis=-1, keepdims=True) + 1e-05)
    normed = centre * inverse
    return (normed, inverse, normed * gain)


def norm_back(upstream, normed, inverse, gain):
    scaled = upstream * gain
    return inverse * (
        scaled
        - jnp.mean(scaled, axis=-1, keepdims=True)
        - normed * jnp.mean(scaled * normed, axis=-1, keepdims=True)
    )


def dot_nt(a, b):
    return lax.dot_general(a, b, (((1,), (1,)), ((), ())), preferred_element_type=F32)


def kernel(
    side,
    pair_ref,
    labels_ref,
    mask_ref,
    norm_gain_ref,
    in_weight_ref,
    gate_weight_ref,
    hidden_gain_ref,
    out_weight_ref,
    bin_weight_ref,
    out_ref,
    left_own,
    right_own,
    left_all,
    right_all,
    acc,
    tri_part,
    tri_in,
    logit_out,
    logit_in,
    label_out,
    label_in,
    gtri,
    gtri_wide,
    gl_part,
    gr_part,
    gl_in,
    gr_in,
    gl_sum,
    gr_sum,
    gl_own,
    gr_own,
    saved,
    s_left1,
    s_right1,
    s_left2,
    s_right2,
    s_tri,
    s_logit,
    s_label,
    s_gtri,
    s_gl1,
    s_gr1,
    s_gl2,
    s_gr2,
    r_left1,
    r_right1,
    r_left2,
    r_right2,
    r_tri,
    r_logit,
    r_label,
    r_gtri,
    r_gl1,
    r_gr1,
    r_gl2,
    r_gr2,
):
    half = side // 2
    x = lax.axis_index("section")
    row = lax.axis_index("row")
    col = lax.axis_index("col")
    zh = row // 2
    core = row % 2
    y = col // side
    zl = col % side
    my_k_core = zl // half
    my_k_slot = zl % half
    diagonal = jnp.logical_and(x == y, zh == zl)

    def device(dx, dy, dzh, dzl, dcore):
        return (dx, dzh * 2 + dcore, dy * side + dzl)

    def send(src, dst, send_sem, recv_sem, target):
        return pltpu.make_async_remote_copy(
            src_ref=src,
            dst_ref=dst,
            send_sem=send_sem,
            recv_sem=recv_sem,
            device_id=target,
            device_id_type=MESH,
        )

    def push(src, dst, send_sem, recv_sem, target, is_self):
        @pl.when(is_self)
        def _():
            pltpu.make_async_copy(src, dst, recv_sem).start()

        @pl.when(jnp.logical_not(is_self))
        def _():
            send(src, dst, send_sem, recv_sem, target).start()

    def drain(src, dst, send_sem, recv_sem, target, is_self):
        @pl.when(jnp.logical_not(is_self))
        def _():
            send(src, dst, send_sem, recv_sem, target).wait_send()

    def arrived(ref, sem):
        pltpu.make_async_copy(ref, ref, sem).wait()

    barrier = pltpu.get_barrier_semaphore()

    def greet(target, is_self):
        @pl.when(jnp.logical_not(is_self))
        def _():
            pl.semaphore_signal(barrier, inc=1, device_id=target, device_id_type=MESH)

    never = x < 0
    for step in range(1, 2 * side):
        other = (zl * 2 + core + step) % (2 * side)
        greet(device(x, y, zh, other // 2, other % 2), never)
    for step in range(1, side):
        greet(device(x, (y + step) % side, zh, zl, core), never)
        greet(device((x + step) % side, y, zh, zl, core), never)
    on_own_path = jnp.logical_and(diagonal, core == my_k_core)
    for there in range(side):
        greet(
            device(y, x, there, zh, my_k_core), jnp.logical_and(on_own_path, there == zh)
        )
    for slot in range(half):
        for there in range(2):
            source = core * half + slot
            greet(
                device(y, x, zl, source, there),
                jnp.logical_and(diagonal, jnp.logical_and(source == zl, there == core)),
            )
    for there in range(2):
        greet(device(y, x, zl, zh, there), jnp.logical_and(diagonal, there == core))
    greetings = 2 * side - 1 + 2 * (side - 1) + 2 * side + 2
    awaited = greetings - 2 * on_own_path.astype(jnp.int32) - diagonal.astype(jnp.int32)

    pair_float = pair_ref[...].astype(F32).reshape(128, 128)
    normed_in, inverse_in, scaled_in = norm_parts(pair_float, norm_gain_ref[...])
    inputs = scaled_in.astype(BF16)
    place = lax.broadcasted_iota(jnp.int32, (128, 256), 0)
    lane = lax.broadcasted_iota(jnp.int32, (128, 256), 1)
    mask_float = mask_ref[...].astype(F32)
    first_row = (x * side + zh) * 16 + core * 8
    first_col = col * 16
    mask_i = jnp.sum(
        jnp.where(lane == first_row + place // 16, mask_float, 0.0), axis=1, keepdims=True
    )
    mask_j = jnp.sum(
        jnp.where(lane == first_col + place % 16, mask_float, 0.0), axis=1, keepdims=True
    )
    pair_mask = mask_i * mask_j
    projected = jnp.dot(inputs, in_weight_ref[...], preferred_element_type=F32)
    sig_a = jax.nn.sigmoid(projected[:, 0:128])
    value_a = projected[:, 128:256]
    sig_b = jax.nn.sigmoid(projected[:, 256:384])
    value_b = projected[:, 384:512]
    right_own[...] = (sig_b * value_b * pair_mask).astype(BF16).reshape(8, 16, 128)
    left_own[...] = (sig_a * value_a * pair_mask).astype(BF16).reshape(8, 16, 128)
    label_out[...] = labels_ref[...].astype(F32)
    pl.semaphore_wait(barrier, awaited)

    def first_right(there):
        return (
            right_own,
            right_all.at[y, my_k_slot, core],
            s_right1.at[there],
            r_right1.at[my_k_slot, core],
            device(y, x, there, zh, my_k_core),
            jnp.logical_and(on_own_path, there == zh),
        )

    def first_left(there):
        return (
            left_own,
            left_all.at[y, my_k_slot, core],
            s_left1.at[there],
            r_left1.at[my_k_slot, core],
            device(x, y, zh, there, my_k_core),
            jnp.logical_and(there == zl, core == my_k_core),
        )

    def labels_to(there):
        return (
            label_out,
            label_in.at[core],
            s_label.at[there],
            r_label.at[core],
            device(y, x, zl, zh, there),
            jnp.logical_and(diagonal, there == core),
        )

    for there in range(side):
        push(*first_right(there))
    for there in range(side):
        push(*first_left(there))
    for there in range(2):
        push(*labels_to(there))

    saved[0] = normed_in
    saved[1] = sig_a
    saved[2] = value_a
    saved[3] = sig_b
    saved[4] = value_b
    saved[5] = jax.nn.sigmoid(jnp.dot(inputs, gate_weight_ref[...], preferred_element_type=F32))
    saved[6] = jnp.broadcast_to(pair_mask, (128, 128))
    saved[7] = jnp.broadcast_to(inverse_in, (128, 128))

    def second_left(slot, step):
        return send(
            left_all.at[y, slot],
            left_all.at[y, slot],
            s_left2.at[slot, step - 1],
            r_left2.at[y, slot],
            device(x, (y + step) % side, zh, zl, core),
        )

    def second_right(slot, step):
        return send(
            right_all.at[x, slot],
            right_all.at[x, slot],
            s_right2.at[slot, step - 1],
            r_right2.at[x, slot],
            device((x + step) % side, y, zh, zl, core),
        )

    for slot in range(half):
        for there in range(2):
            arrived(left_all.at[y, slot, there], r_left1.at[slot, there])
        for step in range(1, side):
            second_left(slot, step).start()
        for there in range(2):
            arrived(right_all.at[x, slot, there], r_right1.at[slot, there])
        for step in range(1, side):
            second_right(slot, step).start()

    acc[...] = jnp.zeros_like(acc)

    def tri_blocks(block, who):
        def body(index, carry):
            i_half = index // 8
            i_low = (index // 4) % 2 * 4
            j_half = (index // 2) % 2
            j_low = index % 2 * 4
            base = index // 4 * 64 + index % 4 * 4
            sums = [[acc[base + a * 16 + b] for b in range(4)] for a in range(4)]
            for slot in range(half):
                lefts = [left_all[who, slot, i_half, i_low + a].astype(F32) for a in range(4)]
                rights = [right_all[who, slot, j_half, j_low + b].astype(F32) for b in range(4)]
                for a in range(4):
                    for b in range(4):
                        product = lefts[a] * rights[b]
                        sums[a][b] = sums[a][b] + (product[0:8] + product[8:16])
            for a in range(4):
                for b in range(4):
                    acc[base + a * 16 + b] = sums[a][b]
            return carry

        lax.fori_loop(block * 8, block * 8 + 8, body, 0)

    def fold(part):
        def body(index, carry):
            at = part * 128 + index * 8
            tri_part[part, pl.ds(index * 8, 8)] = jnp.sum(acc[pl.ds(at, 8)], axis=1)
            return carry

        lax.fori_loop(0, 16, body, 0)

    def tri_copy():
        return send(
            tri_part.at[1 - core],
            tri_in,
            s_tri.at[0],
            r_tri.at[0],
            device(x, y, zh, zl, 1 - core),
        )

    for step in range(side):
        who = (y + step) % side
        if step > 0:
            for slot in range(half):
                arrived(left_all.at[who, slot], r_left2.at[who, slot])

        @pl.when(who != x)
        def _():
            for slot in range(half):
                arrived(right_all.at[who, slot], r_right2.at[who, slot])

        tri_blocks(1 - core, who)
        if step == side - 1:
            fold(1 - core)
            tri_copy().start()
        tri_blocks(core, who)
    fold(core)
    arrived(tri_in, r_tri.at[0])
    triangle = tri_part[core] + tri_in[...]

    hidden_gain = hidden_gain_ref[...]
    normed_t, inverse_t, scaled_t = norm_parts(triangle, hidden_gain)
    update = jnp.dot(scaled_t.astype(BF16), out_weight_ref[...], preferred_element_type=F32)
    gate_out = saved[5]
    pair_out = (pair_ref[...].astype(F32).reshape(128, 128) + gate_out * update).astype(BF16)
    logits = jnp.dot(pair_out, bin_weight_ref[...], preferred_element_type=F32)
    logits = logits.astype(BF16).astype(F32)
    blocks = logits.reshape(8, 2, 8, 64)
    for there in range(2):
        logit_out[there] = blocks[:, there].reshape(64, 64).astype(BF16)

    def logits_to(there):
        return (
            logit_out.at[there],
            logit_in.at[core],
            s_logit.at[there],
            r_logit.at[core],
            device(y, x, zl, zh, there),
            jnp.logical_and(diagonal, there == core),
        )

    for there in range(2):
        push(*logits_to(there))

    for there in range(2):
        arrived(label_in.at[there], r_label.at[there])
    place16 = lax.broadcasted_iota(jnp.int32, (128, 16), 0)
    lane16 = lax.broadcasted_iota(jnp.int32, (128, 16), 1)
    place8 = lax.broadcasted_iota(jnp.int32, (128, 8), 0)
    lane8 = lax.broadcasted_iota(jnp.int32, (128, 8), 1)
    spread = jnp.dot(
        (lane8 == place8 // 16).astype(F32), label_out[...], preferred_element_type=F32
    )
    label = jnp.sum(jnp.where(lane16 == place16 % 16, spread, 0.0), axis=1, keepdims=True)
    spread = jnp.dot(
        (lane16 == place16 % 16).astype(F32),
        label_in[...].reshape(16, 16),
        preferred_element_type=F32,
    )
    label_mirror = jnp.sum(
        jnp.where(lane16 == core * 8 + place16 // 16, spread, 0.0), axis=1, keepdims=True
    )
    bins = lax.broadcasted_iota(jnp.int32, (128, 64), 1)
    onehot = (label.astype(jnp.int32) == bins).astype(F32)
    onehot_mirror = (label_mirror.astype(jnp.int32) == bins).astype(F32)
    at_row = lax.broadcasted_iota(jnp.int32, (128, 128), 0)
    at_lane = lax.broadcasted_iota(jnp.int32, (128, 128), 1)
    turn = at_lane == (at_row // 8) % 2 * 64 + at_row % 8 * 8 + at_row // 16
    turn = turn.astype(F32).astype(BF16)
    mask_wide = saved[6]
    pair_mask = mask_wide[:, 0:64]

    for there in range(2):
        arrived(logit_in.at[there], r_logit.at[there])
    mirrored = jnp.dot(turn, logit_in[...].reshape(128, 64), preferred_element_type=F32)
    weights = jnp.exp(logits + mirrored)
    probs = weights / jnp.sum(weights, axis=-1, keepdims=True)
    grad_bins = (pair_mask * (probs - onehot)).astype(BF16).astype(F32)
    grad_mirror = (pair_mask * (probs - onehot_mirror)).astype(BF16).astype(F32)
    grad_sym = (grad_bins + grad_mirror).astype(BF16)
    grad_out = dot_nt(grad_sym, bin_weight_ref[...])
    grad_update = (grad_out * gate_out).astype(BF16)
    grad_scaled = dot_nt(grad_update, out_weight_ref[...])
    grad_triangle = norm_back(grad_scaled, normed_t, inverse_t, hidden_gain)
    gtri[core] = grad_triangle.astype(BF16)

    def gtri_copy():
        return send(
            gtri.at[core],
            gtri.at[core],
            s_gtri.at[0],
            r_gtri.at[core],
            device(x, y, zh, zl, 1 - core),
        )

    gtri_copy().start()
    grad_gate = (grad_out * update * gate_out * (1.0 - gate_out)).astype(BF16)
    saved[8] = grad_out
    saved[9] = dot_nt(grad_gate, gate_weight_ref[...])

    def widen(part):
        def body(index, carry):
            rows = gtri[part, pl.ds(index * 16, 16)].astype(F32)
            for a in range(16):
                gtri_wide[part * 128 + index * 16 + a] = jnp.broadcast_to(
                    rows[a : a + 1], (8, 128)
                )
            return carry

        lax.fori_loop(0, 8, body, 0)

    widen(core)
    arrived(gtri.at[1 - core], r_gtri.at[1 - core])
    widen(1 - core)

    def partial(out, source, who, slot, across, along):
        def body(part, carry):
            low = [jnp.zeros((8, 128), F32) for _ in range(8)]
            high = [jnp.zeros((8, 128), F32) for _ in range(8)]
            for n in range(16):
                tile = source[who, slot, n // 8, n % 8].astype(F32)
                for a in range(8):
                    factor = gtri_wide[(part * 8 + a) * across + n * along]
                    low[a] = low[a] + factor * tile[0:8]
                    high[a] = high[a] + factor * tile[8:16]
            for a in range(8):
                out[who, slot, part, a] = jnp.concatenate([low[a], high[a]], axis=0).astype(BF16)
            return carry

        lax.fori_loop(0, 2, body, 0)

    def third_left(slot, step):
        who = (y + step) % side
        return send(
            gl_part.at[who, slot],
            gl_in.at[y, slot],
            s_gl1.at[slot, step - 1],
            r_gl1.at[y, slot],
            device(x, who, zh, zl, core),
        )

    def third_right(slot, step):
        who = (x + step) % side
        return send(
            gr_part.at[who, slot],
            gr_in.at[x, slot],
            s_gr1.at[slot, step - 1],
            r_gr1.at[x, slot],
            device(who, y, zh, zl, core),
        )

    def partial_step(index, carry):
        slot = index // (side - 1)
        step = index % (side - 1) + 1
        partial(gr_part, left_all, (x + step) % side, slot, 1, 16)
        third_right(slot, step).start()
        partial(gl_part, right_all, (y + step) % side, slot, 16, 1)
        third_left(slot, step).start()
        return carry

    lax.fori_loop(0, half * (side - 1), partial_step, 0)

    def own_step(slot, carry):
        partial(gr_part, left_all, x, slot, 1, 16)
        partial(gl_part, right_all, y, slot, 16, 1)
        return carry

    lax.fori_loop(0, half, own_step, 0)

    def fourth_left(slot, there):
        owner = core * half + slot
        return (
            gl_sum.at[slot, there],
            gl_own.at[zl],
            s_gl2.at[slot, there],
            r_gl2.at[zl],
            device(x, y, zh, owner, there),
            jnp.logical_and(owner == zl, there == core),
        )

    def fourth_right(slot, there):
        owner = core * half + slot
        return (
            gr_sum.at[slot, there],
            gr_own.at[zh],
            s_gr2.at[slot, there],
            r_gr2.at[zh],
            device(y, x, zl, owner, there),
            jnp.logical_and(diagonal, jnp.logical_and(owner == zl, there == core)),
        )

    def sum_leg(total, part, come, sems, me, slot):
        for step in range(1, side):
            who = (me + step) % side
            arrived(come.at[who, slot], sems.at[who, slot])
        for there in range(2):
            value = part[me, slot, there].astype(F32)
            for step in range(1, side):
                value = value + come[(me + step) % side, slot, there].astype(F32)
            total[slot, there] = value.astype(BF16)

    for slot in range(half):
        sum_leg(gr_sum, gr_part, gr_in, r_gr1, x, slot)
        for there in range(2):
            push(*fourth_right(slot, there))
        sum_leg(gl_sum, gl_part, gl_in, r_gl1, y, slot)
        for there in range(2):
            push(*fourth_left(slot, there))

    def total_of(own, sems):
        value = None
        for there in range(side):
            arrived(own.at[there], sems.at[there])
            term = own[there].astype(F32)
            value = term if value is None else value + term
        return value.reshape(128, 128)

    grad_left = total_of(gl_own, r_gl2)
    sig_a = saved[1]
    value_a = saved[2]
    masked = grad_left * mask_wide
    proj_0 = (masked * value_a * sig_a * (1.0 - sig_a)).astype(BF16)
    proj_1 = (masked * sig_a).astype(BF16)
    grad_right = total_of(gr_own, r_gr2)
    sig_b = saved[3]
    value_b = saved[4]
    masked = grad_right * mask_wide
    proj_2 = (masked * value_b * sig_b * (1.0 - sig_b)).astype(BF16)
    proj_3 = (masked * sig_b).astype(BF16)
    grad_proj = jnp.concatenate([proj_0, proj_1, proj_2, proj_3], axis=-1)
    grad_inputs = dot_nt(grad_proj, in_weight_ref[...]) + saved[9]
    result = saved[8] + norm_back(grad_inputs, saved[0], saved[7], norm_gain_ref[...])
    out_ref[...] = result.astype(BF16).reshape(8, 16, 128)

    for there in range(side):
        drain(*first_right(there))
        drain(*first_left(there))
    for there in range(2):
        drain(*labels_to(there))
        drain(*logits_to(there))
    tri_copy().wait_send()
    gtri_copy().wait_send()
    for slot in range(half):
        for step in range(1, side):
            second_left(slot, step).wait_send()
            second_right(slot, step).wait_send()
            third_left(slot, step).wait_send()
            third_right(slot, step).wait_send()
        for there in range(2):
            drain(*fourth_left(slot, there))
            drain(*fourth_right(slot, there))


def local(
    pair,
    labels,
    residue_mask,
    norm_gain,
    in_weight,
    gate_weight,
    hidden_gain,
    out_weight,
    bin_weight,
):
    side = lax.axis_size("section")
    half = side // 2
    tile = (8, 16, 128)
    sems = [
        (side,),
        (side,),
        (half, side - 1),
        (half, side - 1),
        (1,),
        (2,),
        (2,),
        (1,),
        (half, side - 1),
        (half, side - 1),
        (half, 2),
        (half, 2),
        (half, 2),
        (half, 2),
        (side, half),
        (side, half),
        (1,),
        (2,),
        (2,),
        (2,),
        (side, half),
        (side, half),
        (side,),
        (side,),
    ]
    gathered = pltpu.VMEM((side, half, 2) + tile, BF16)
    residues = residue_mask.shape[0]
    if residues < 256:
        residue_mask = jnp.pad(residue_mask, (0, 256 - residues))
    return pl.pallas_call(
        functools.partial(kernel, side),
        out_shape=jax.ShapeDtypeStruct(tile, BF16),
        in_specs=[pl.BlockSpec(memory_space=pltpu.VMEM)] * 9,
        out_specs=pl.BlockSpec(memory_space=pltpu.VMEM),
        scratch_shapes=[
            pltpu.VMEM(tile, BF16),
            pltpu.VMEM(tile, BF16),
            gathered,
            gathered,
            pltpu.VMEM((256, 8, 128), F32),
            pltpu.VMEM((2, 128, 128), F32),
            pltpu.VMEM((128, 128), F32),
            pltpu.VMEM((2, 64, 64), BF16),
            pltpu.VMEM((2, 64, 64), BF16),
            pltpu.VMEM((8, 16), F32),
            pltpu.VMEM((2, 8, 16), F32),
            pltpu.VMEM((2, 128, 128), BF16),
            pltpu.VMEM((256, 8, 128), F32),
            gathered,
            gathered,
            gathered,
            gathered,
            pltpu.VMEM((half, 2) + tile, BF16),
            pltpu.VMEM((half, 2) + tile, BF16),
            pltpu.VMEM((side,) + tile, BF16),
            pltpu.VMEM((side,) + tile, BF16),
            pltpu.VMEM((10, 128, 128), F32),
        ]
        + [pltpu.SemaphoreType.DMA(shape) for shape in sems],
        compiler_params=pltpu.CompilerParams(
            collective_id=0, has_side_effects=True, vmem_limit_bytes=32 * 1024 * 1024
        ),
    )(
        pair,
        labels,
        residue_mask[None, :],
        norm_gain[None, :],
        in_weight,
        gate_weight,
        hidden_gain[None, :],
        out_weight,
        bin_weight,
    )


def solution(mesh):
    placed = (
        P(("section", "row"), "col", None),
        P(("section", "row"), "col"),
        P(),
        P(),
        P(),
        P(),
        P(),
        P(),
        P(),
    )
    return jax.shard_map(
        local,
        mesh=mesh,
        in_specs=placed,
        out_specs=P(("section", "row"), "col", None),
        check_vma=False,
    )
```

time: 558 us -> 76.5 us (0.14)
  the two profiles are of different devices: /device:TPU:32 before, /device:TPU:1 now
where the time goes in v1:
time: 76.5 us; the launch traced here: 76.2 us
  Pallas kernels  72.2 us (94%)
  local copies, waits for them, and re-layouts  3.92 us (5%)
    pallas_call x1, Pallas kernels, local(): pl.pallas_call(functools.partial(kernel, side), out_shape=jax.ShapeDtypeS...  72.2 us
    unnamed x18, local copies, waits for them, and re-layouts  3.92 us

profile of v1, /device:TPU:1, one launch (start us, length us, event | category | flops | bytes accessed | tf_op | source)
XLA Modules:
  0.0 76.2 jit_solution(6590358791052460200)
XLA Ops:
  0.0 0.0 copy-start.1
  0.0 0.0 copy-start.4
  0.0 0.0 copy-start.5
  0.0 0.0 copy-start.6
  0.0 0.0 copy-start.7
  0.0 0.9 %copy.10.bin_weight_ref = bf16[128,64]{1,0:T(8,128)(2,1)S(1)} copy(bf16[128,64]{0,1:T(8,128)(2,1)} %param.17) | data formatting | bytes 32768 | tf_op args[8]
  0.9 0.0 copy-done.1
  0.9 0.0 copy-done.4
  0.9 0.0 copy-done.5
  0.9 0.0 copy-done.6
  0.9 0.0 copy-done.7
  1.0 0.0 copy-start
  1.0 0.9 %copy-done = bf16[128,512]{1,0:T(8,128)(2,1)S(1)} copy-done((bf16[128,512]{1,0:T(8,128)(2,1)S(1)}, bf16[128,512]{1,0:T(8,128)(2,1)}, u32[]{:S(2)}) %copy-start) | copy-done | bytes 131096
  1.9 0.0 copy-start.2
  1.9 0.8 copy-done.2
  2.6 0.0 copy-start.3
  2.6 0.8 copy-done.3
  3.4 72.2 %shard_map.91 = bf16[8,16,128]{2,1,0:T(8,128)(2,1)S(1)} custom-call(bf16[8,16,128]{2,1,0:T(8,128)(2,1)S(1)} %copy-done.1, s32[8,16]{1,0:T(8,128)S(1)} %copy-done.4, s32[1,256]{1,0:T(1,128)S(1)} %bitcast.3, f32[1,128]{1,0:T(1,128)S(1)} %bitcast.4, bf16[128,512]{1,0:T(8,128)(2,1)S(1)} %copy-done, bf16[128,128]{1,0:T(8,128)(2,1)S(1)} %copy-done.2, ...), custom_call_target="tpu_custom_call" | custom-call | tf_op jit(solution)/shard_map/pallas_call | solution.py:604
  75.6 0.6 copy.12
Async XLA Ops:
  0.0 0.9 %copy-start.1 = (bf16[8,16,128]{2,1,0:T(8,128)(2,1)S(1)}, bf16[8,16,128]{2,1,0:T(8,128)(2,1)}, u32[]{:S(2)}) copy-start(bf16[8,16,128]{2,1,0:T(8,128)(2,1)} %pair_ref.1) | copy-start | bytes 98308
  0.0 0.9 %copy-start.4 = (s32[8,16]{1,0:T(8,128)S(1)}, s32[8,16]{1,0:T(8,128)}, u32[]{:S(2)}) copy-start(s32[8,16]{1,0:T(8,128)} %labels_ref.1) | copy-start | bytes 1540
  0.0 0.9 %copy-start.5 = (s32[256]{0:T(256)S(1)}, s32[256]{0:T(256)}, u32[]{:S(2)}) copy-start(s32[256]{0:T(256)} %param.11) | copy-start | bytes 3076
  0.0 0.9 %copy-start.6 = (f32[128]{0:T(128)S(1)}, f32[128]{0:T(128)}, u32[]{:S(2)}) copy-start(f32[128]{0:T(128)} %param.12) | copy-start | bytes 1540
  0.0 0.9 %copy-start.7 = (f32[128]{0:T(128)S(1)}, f32[128]{0:T(128)}, u32[]{:S(2)}) copy-start(f32[128]{0:T(128)} %param.15) | copy-start | bytes 1540
  1.0 0.9 %copy-start = (bf16[128,512]{1,0:T(8,128)(2,1)S(1)}, bf16[128,512]{1,0:T(8,128)(2,1)}, u32[]{:S(2)}) copy-start(bf16[128,512]{1,0:T(8,128)(2,1)} %in_weight_ref.1) | copy-start | bytes 393220
  1.9 0.8 copy-start.2
  2.6 0.8 copy-start.3

commit v2 on v1

--- a/solution.py
+++ b/solution.py
@@ -34,6 +34,16 @@
 
 def kernel(
     side,
+    pair_hbm,
+    labels_hbm,
+    mask_hbm,
+    norm_gain_hbm,
+    in_weight_hbm,
+    gate_weight_hbm,
+    hidden_gain_hbm,
+    out_weight_hbm,
+    bin_weight_hbm,
+    out_ref,
     pair_ref,
     labels_ref,
     mask_ref,
@@ -43,7 +53,7 @@
     hidden_gain_ref,
     out_weight_ref,
     bin_weight_ref,
-    out_ref,
+    loaded,
     left_own,
     right_own,
     left_all,
@@ -55,12 +65,12 @@
     logit_in,
     label_out,
     label_in,
+    left_x,
     gtri,
-    gtri_wide,
+    gtri_float,
     gl_part,
-    gr_part,
     gl_in,
-    gr_in,
+    gr_acc,
     gl_sum,
     gr_sum,
     gl_own,
@@ -73,9 +83,9 @@
     s_tri,
     s_logit,
     s_label,
+    s_left_x,
     s_gtri,
     s_gl1,
-    s_gr1,
     s_gl2,
     s_gr2,
     r_left1,
@@ -85,9 +95,9 @@
     r_tri,
     r_logit,
     r_label,
+    r_left_x,
     r_gtri,
     r_gl1,
-    r_gr1,
     r_gl2,
     r_gr2,
 ):
@@ -103,6 +113,12 @@
     my_k_slot = zl % half
     diagonal = jnp.logical_and(x == y, zh == zl)
 
+    def turned(a, b):
+        return (2 * a + side // 2 - b + side) % side
+
+    mine = turned(y, x)
+    meet = turned(x, y)
+
     def device(dx, dy, dzh, dzl, dcore):
         return (dx, dzh * 2 + dcore, dy * side + dzl)
 
@@ -135,35 +151,58 @@
 
     barrier = pltpu.get_barrier_semaphore()
 
-    def greet(target, is_self):
-        @pl.when(jnp.logical_not(is_self))
-        def _():
+    operands = (
+        (pair_hbm, pair_ref),
+        (norm_gain_hbm, norm_gain_ref),
+        (in_weight_hbm, in_weight_ref),
+        (mask_hbm, mask_ref),
+        (labels_hbm, labels_ref),
+        (gate_weight_hbm, gate_weight_ref),
+        (hidden_gain_hbm, hidden_gain_ref),
+        (out_weight_hbm, out_weight_ref),
+        (bin_weight_hbm, bin_weight_ref),
+    )
+
+    def load(index):
+        return pltpu.make_async_copy(*operands[index], loaded.at[index])
+
+    def greet(target, is_self=None):
+        def signal():
             pl.semaphore_signal(barrier, inc=1, device_id=target, device_id_type=MESH)
 
-    never = x < 0
-    for step in range(1, 2 * side):
-        other = (zl * 2 + core + step) % (2 * side)
-        greet(device(x, y, zh, other // 2, other % 2), never)
-    for step in range(1, side):
-        greet(device(x, (y + step) % side, zh, zl, core), never)
-        greet(device((x + step) % side, y, zh, zl, core), never)
-    on_own_path = jnp.logical_and(diagonal, core == my_k_core)
+        if is_self is None:
+            signal()
+        else:
+            pl.when(jnp.logical_not(is_self))(signal)
+
+    on_own_path = jnp.logical_and(
+        jnp.logical_and(x == y, meet == x), jnp.logical_and(zh == zl, core == my_k_core)
+    )
     for there in range(side):
         greet(
-            device(y, x, there, zh, my_k_core), jnp.logical_and(on_own_path, there == zh)
+            device(meet, x, there, zh, my_k_core), jnp.logical_and(on_own_path, there == zh)
         )
     for slot in range(half):
         for there in range(2):
             source = core * half + slot
             greet(
-                device(y, x, zl, source, there),
-                jnp.logical_and(diagonal, jnp.logical_and(source == zl, there == core)),
+                device(y, mine, zl, source, there),
+                jnp.logical_and(on_own_path, jnp.logical_and(source == zl, there == core)),
             )
-    for there in range(2):
-        greet(device(y, x, zl, zh, there), jnp.logical_and(diagonal, there == core))
-    greetings = 2 * side - 1 + 2 * (side - 1) + 2 * side + 2
-    awaited = greetings - 2 * on_own_path.astype(jnp.int32) - diagonal.astype(jnp.int32)
-
+    for index in range(9):
+        load(index).start()
+    for step in range(1, 2 * side):
+        other = (zl * 2 + core + step) % (2 * side)
+        greet(device(x, y, zh, other // 2, other % 2))
+    for step in range(1, side):
+        greet(device(x, (y + step) % side, zh, zl, core))
+        greet(device((x + step) % side, y, zh, zl, core))
+        greet(device((x + step) % side, y, zh, zl, 1 - core))
+    greetings = 2 * side - 1 + 3 * (side - 1) + 2 * side
+    awaited = greetings - 2 * on_own_path.astype(jnp.int32)
+
+    for index in range(5):
+        load(index).wait()
     pair_float = pair_ref[...].astype(F32).reshape(128, 128)
     normed_in, inverse_in, scaled_in = norm_parts(pair_float, norm_gain_ref[...])
     inputs = scaled_in.astype(BF16)
@@ -195,7 +234,7 @@
             right_all.at[y, my_k_slot, core],
             s_right1.at[there],
             r_right1.at[my_k_slot, core],
-            device(y, x, there, zh, my_k_core),
+            device(meet, x, there, zh, my_k_core),
             jnp.logical_and(on_own_path, there == zh),
         )
 
@@ -219,12 +258,14 @@
             jnp.logical_and(diagonal, there == core),
         )
 
-    for there in range(side):
-        push(*first_right(there))
+    my_turn = my_k_slot * 2 + core
+    for phase in range(side):
+        push(*first_right((my_turn + phase) % side))
     for there in range(side):
         push(*first_left(there))
-    for there in range(2):
-        push(*labels_to(there))
+
+    for index in range(5, 9):
+        load(index).wait()
 
     saved[0] = normed_in
     saved[1] = sig_a
@@ -244,12 +285,16 @@
             device(x, (y + step) % side, zh, zl, core),
         )
 
-    def second_right(slot, step):
+    def turn_of(phase):
+        index = (zh - phase + side) % side
+        return index // 2, index % 2
+
+    def second_right(slot, part, step):
         return send(
-            right_all.at[x, slot],
-            right_all.at[x, slot],
-            s_right2.at[slot, step - 1],
-            r_right2.at[x, slot],
+            right_all.at[mine, slot, part],
+            right_all.at[mine, slot, part],
+            s_right2.at[slot, part, step - 1],
+            r_right2.at[mine, slot, part],
             device((x + step) % side, y, zh, zl, core),
         )
 
@@ -258,22 +303,22 @@
             arrived(left_all.at[y, slot, there], r_left1.at[slot, there])
         for step in range(1, side):
             second_left(slot, step).start()
-        for there in range(2):
-            arrived(right_all.at[x, slot, there], r_right1.at[slot, there])
+
+    def forward(phase):
+        slot, part = turn_of(phase)
+        arrived(right_all.at[mine, slot, part], r_right1.at[slot, part])
         for step in range(1, side):
-            second_right(slot, step).start()
+            second_right(slot, part, step).start()
 
     acc[...] = jnp.zeros_like(acc)
 
-    def tri_blocks(block, who):
+    def tri_blocks(i_half, slot, j_half):
         def body(index, carry):
-            i_half = index // 8
-            i_low = (index // 4) % 2 * 4
-            j_half = (index // 2) % 2
+            i_low = index // 2 * 4
             j_low = index % 2 * 4
-            base = index // 4 * 64 + index % 4 * 4
+            base = (i_half * 8 + i_low) * 16 + j_half * 8 + j_low
             sums = [[acc[base + a * 16 + b] for b in range(4)] for a in range(4)]
-            for slot in range(half):
+            for who in range(side):
                 lefts = [left_all[who, slot, i_half, i_low + a].astype(F32) for a in range(4)]
                 rights = [right_all[who, slot, j_half, j_low + b].astype(F32) for b in range(4)]
                 for a in range(4):
@@ -285,7 +330,7 @@
                     acc[base + a * 16 + b] = sums[a][b]
             return carry
 
-        lax.fori_loop(block * 8, block * 8 + 8, body, 0)
+        lax.fori_loop(0, 4, body, 0)
 
     def fold(part):
         def body(index, carry):
@@ -304,22 +349,27 @@
             device(x, y, zh, zl, 1 - core),
         )
 
-    for step in range(side):
-        who = (y + step) % side
-        if step > 0:
-            for slot in range(half):
-                arrived(left_all.at[who, slot], r_left2.at[who, slot])
-
-        @pl.when(who != x)
-        def _():
-            for slot in range(half):
-                arrived(right_all.at[who, slot], r_right2.at[who, slot])
-
-        tri_blocks(1 - core, who)
-        if step == side - 1:
+    forward(0)
+    for phase in range(side):
+        if phase < side - 1:
+            forward(phase + 1)
+        slot, part = turn_of(phase)
+        if phase == 0:
+            for step in range(1, side):
+                for there in range(half):
+                    who = (y + step) % side
+                    arrived(left_all.at[who, there], r_left2.at[who, there])
+        for step in range(1, side):
+            who = (mine + step) % side
+            arrived(right_all.at[who, slot, part], r_right2.at[who, slot, part])
+        if phase == side - 1:
+            for there in range(2):
+                push(*labels_to(there))
+        tri_blocks(1 - core, slot, part)
+        if phase == side - 1:
             fold(1 - core)
             tri_copy().start()
-        tri_blocks(core, who)
+        tri_blocks(core, slot, part)
     fold(core)
     arrived(tri_in, r_tri.at[0])
     triangle = tri_part[core] + tri_in[...]
@@ -329,7 +379,7 @@
     update = jnp.dot(scaled_t.astype(BF16), out_weight_ref[...], preferred_element_type=F32)
     gate_out = saved[5]
     pair_out = (pair_ref[...].astype(F32).reshape(128, 128) + gate_out * update).astype(BF16)
-    logits = jnp.dot(pair_out, bin_weight_ref[...], preferred_element_type=F32)
+    logits = dot_nt(pair_out, bin_weight_ref[...])
     logits = logits.astype(BF16).astype(F32)
     blocks = logits.reshape(8, 2, 8, 64)
     for there in range(2):
@@ -347,6 +397,20 @@
 
     for there in range(2):
         push(*logits_to(there))
+
+    def left_to(step):
+        who = (x + step) % side
+        return send(
+            left_all.at[turned(y, who)],
+            left_x.at[x],
+            s_left_x.at[step - 1],
+            r_left_x.at[x],
+            device(who, y, zh, zl, core),
+        )
+
+    for step in range(1, side):
+        left_to(step).start()
+    pltpu.make_async_copy(left_all.at[mine], left_x.at[x], r_left_x.at[x]).start()
 
     for there in range(2):
         arrived(label_in.at[there], r_label.at[there])
@@ -384,94 +448,81 @@
     grad_bins = (pair_mask * (probs - onehot)).astype(BF16).astype(F32)
     grad_mirror = (pair_mask * (probs - onehot_mirror)).astype(BF16).astype(F32)
     grad_sym = (grad_bins + grad_mirror).astype(BF16)
-    grad_out = dot_nt(grad_sym, bin_weight_ref[...])
+    grad_out = jnp.dot(grad_sym, bin_weight_ref[...], preferred_element_type=F32)
     grad_update = (grad_out * gate_out).astype(BF16)
     grad_scaled = dot_nt(grad_update, out_weight_ref[...])
     grad_triangle = norm_back(grad_scaled, normed_t, inverse_t, hidden_gain)
-    gtri[core] = grad_triangle.astype(BF16)
-
-    def gtri_copy():
+    gtri[x, core] = grad_triangle.astype(BF16)
+
+    def gtri_to(step):
+        other = (x * 2 + core + step) % (2 * side)
         return send(
-            gtri.at[core],
-            gtri.at[core],
-            s_gtri.at[0],
-            r_gtri.at[core],
-            device(x, y, zh, zl, 1 - core),
-        )
-
-    gtri_copy().start()
+            gtri.at[x, core],
+            gtri.at[x, core],
+            s_gtri.at[step - 1],
+            r_gtri.at[x, core],
+            device(other // 2, y, zh, zl, other % 2),
+        )
+
+    for step in range(1, 2 * side):
+        gtri_to(step).start()
     grad_gate = (grad_out * update * gate_out * (1.0 - gate_out)).astype(BF16)
     saved[8] = grad_out
     saved[9] = dot_nt(grad_gate, gate_weight_ref[...])
 
-    def widen(part):
-        def body(index, carry):
-            rows = gtri[part, pl.ds(index * 16, 16)].astype(F32)
-            for a in range(16):
-                gtri_wide[part * 128 + index * 16 + a] = jnp.broadcast_to(
-                    rows[a : a + 1], (8, 128)
-                )
-            return carry
-
-        lax.fori_loop(0, 8, body, 0)
-
-    widen(core)
-    arrived(gtri.at[1 - core], r_gtri.at[1 - core])
-    widen(1 - core)
-
-    def partial(out, source, who, slot, across, along):
-        def body(part, carry):
-            low = [jnp.zeros((8, 128), F32) for _ in range(8)]
-            high = [jnp.zeros((8, 128), F32) for _ in range(8)]
-            for n in range(16):
-                tile = source[who, slot, n // 8, n % 8].astype(F32)
-                for a in range(8):
-                    factor = gtri_wide[(part * 8 + a) * across + n * along]
-                    low[a] = low[a] + factor * tile[0:8]
-                    high[a] = high[a] + factor * tile[8:16]
+    def widen(who, part):
+        gtri_float[who, part] = gtri[who, part].astype(F32)
+
+    widen(x, core)
+    arrived(gtri.at[x, 1 - core], r_gtri.at[x, 1 - core])
+    widen(x, 1 - core)
+
+    def products(sums, tile_of, factor_of):
+        low, high = list(sums[0:8]), list(sums[8:16])
+        for n in range(16):
+            tile = tile_of(n).astype(F32)
             for a in range(8):
-                out[who, slot, part, a] = jnp.concatenate([low[a], high[a]], axis=0).astype(BF16)
-            return carry
-
-        lax.fori_loop(0, 2, body, 0)
-
-    def third_left(slot, step):
+                factor = jnp.broadcast_to(factor_of(n, a), (8, 128))
+                low[a] = low[a] + factor * tile[0:8]
+                high[a] = high[a] + factor * tile[8:16]
+        return low + high
+
+    nothing = [jnp.zeros((8, 128), F32) for _ in range(16)]
+
+    def partial_left(who, slot, part):
+        sums = products(
+            nothing,
+            lambda n: right_all[who, slot, n // 8, n % 8],
+            lambda n, a: gtri_float[x, part, pl.ds(a * 16 + n, 1)],
+        )
+        for a in range(8):
+            gl_part[who, slot, part, a] = jnp.concatenate(
+                [sums[a], sums[a + 8]], axis=0
+            ).astype(BF16)
+
+    def third_left(slot, part, step):
         who = (y + step) % side
         return send(
-            gl_part.at[who, slot],
-            gl_in.at[y, slot],
-            s_gl1.at[slot, step - 1],
-            r_gl1.at[y, slot],
+            gl_part.at[who, slot, part],
+            gl_in.at[y, slot, part],
+            s_gl1.at[slot, part, step - 1],
+            r_gl1.at[y, slot, part],
             device(x, who, zh, zl, core),
         )
 
-    def third_right(slot, step):
-        who = (x + step) % side
-        return send(
-            gr_part.at[who, slot],
-            gr_in.at[x, slot],
-            s_gr1.at[slot, step - 1],
-            r_gr1.at[x, slot],
-            device(who, y, zh, zl, core),
-        )
-
-    def partial_step(index, carry):
-        slot = index // (side - 1)
-        step = index % (side - 1) + 1
-        partial(gr_part, left_all, (x + step) % side, slot, 1, 16)
-        third_right(slot, step).start()
-        partial(gl_part, right_all, (y + step) % side, slot, 16, 1)
-        third_left(slot, step).start()
-        return carry
-
-    lax.fori_loop(0, half * (side - 1), partial_step, 0)
-
-    def own_step(slot, carry):
-        partial(gr_part, left_all, x, slot, 1, 16)
-        partial(gl_part, right_all, y, slot, 16, 1)
-        return carry
-
-    lax.fori_loop(0, half, own_step, 0)
+    def partials_left(phase):
+        slot, part = turn_of(phase)
+
+        def body(step, carry):
+            partial_left((y + step) % side, slot, part)
+
+            @pl.when(step < side)
+            def _():
+                third_left(slot, part, step).start()
+
+            return carry
+
+        lax.fori_loop(1, side + 1, body, 0)
 
     def fourth_left(slot, there):
         owner = core * half + slot
@@ -491,27 +542,60 @@
             gr_own.at[zh],
             s_gr2.at[slot, there],
             r_gr2.at[zh],
-            device(y, x, zl, owner, there),
-            jnp.logical_and(diagonal, jnp.logical_and(owner == zl, there == core)),
-        )
-
-    def sum_leg(total, part, come, sems, me, slot):
+            device(y, mine, zl, owner, there),
+            jnp.logical_and(on_own_path, jnp.logical_and(owner == zl, there == core)),
+        )
+
+    for phase in range(side):
+        partials_left(phase)
+
+    order = sorted(range(side), key=lambda step: min(step, side - step))
+    for step in order:
+        who = (x + step) % side
+        if step > 0:
+            for there in range(2):
+                arrived(gtri.at[who, there], r_gtri.at[who, there])
+                widen(who, there)
+        arrived(left_x.at[who], r_left_x.at[who])
+
+        def right_block(index, carry, step=step, who=who):
+            slot = index // 2
+            part = index % 2
+            if step == 0:
+                sums = nothing
+            else:
+                sums = [gr_acc[index, a] for a in range(16)]
+            sums = products(
+                sums,
+                lambda n: left_x[who, slot, n // 8, n % 8],
+                lambda n, a: gtri_float[who, n // 8, pl.ds(n % 8 * 16 + part * 8 + a, 1)],
+            )
+            if step == order[-1]:
+                for a in range(8):
+                    gr_sum[slot, part, a] = jnp.concatenate(
+                        [sums[a], sums[a + 8]], axis=0
+                    ).astype(BF16)
+                push(*fourth_right(slot, part))
+            else:
+                for a in range(16):
+                    gr_acc[index, a] = sums[a]
+            return carry
+
+        lax.fori_loop(0, 2 * half, right_block, 0)
+
+    def sums_left(phase):
+        slot, there = turn_of(phase)
         for step in range(1, side):
-            who = (me + step) % side
-            arrived(come.at[who, slot], sems.at[who, slot])
-        for there in range(2):
-            value = part[me, slot, there].astype(F32)
-            for step in range(1, side):
-                value = value + come[(me + step) % side, slot, there].astype(F32)
-            total[slot, there] = value.astype(BF16)
-
-    for slot in range(half):
-        sum_leg(gr_sum, gr_part, gr_in, r_gr1, x, slot)
-        for there in range(2):
-            push(*fourth_right(slot, there))
-        sum_leg(gl_sum, gl_part, gl_in, r_gl1, y, slot)
-        for there in range(2):
-            push(*fourth_left(slot, there))
+            who = (y + step) % side
+            arrived(gl_in.at[who, slot, there], r_gl1.at[who, slot, there])
+        value = gl_part[y, slot, there].astype(F32)
+        for step in range(1, side):
+            value = value + gl_in[(y + step) % side, slot, there].astype(F32)
+        gl_sum[slot, there] = value.astype(BF16)
+        push(*fourth_left(slot, there))
+
+    for phase in range(side):
+        sums_left(phase)
 
     def total_of(own, sems):
         value = None
@@ -545,14 +629,17 @@
         drain(*labels_to(there))
         drain(*logits_to(there))
     tri_copy().wait_send()
-    gtri_copy().wait_send()
+    for step in range(1, side):
+        left_to(step).wait_send()
+    for step in range(1, 2 * side):
+        gtri_to(step).wait_send()
     for slot in range(half):
         for step in range(1, side):
             second_left(slot, step).wait_send()
-            second_right(slot, step).wait_send()
-            third_left(slot, step).wait_send()
-            third_right(slot, step).wait_send()
         for there in range(2):
+            for step in range(1, side):
+                second_right(slot, there, step).wait_send()
+                third_left(slot, there, step).wait_send()
             drain(*fourth_left(slot, there))
             drain(*fourth_right(slot, there))
 
@@ -575,25 +662,25 @@
         (side,),
         (side,),
         (half, side - 1),
-        (half, side - 1),
+        (half, 2, side - 1),
         (1,),
         (2,),
         (2,),
-        (1,),
-        (half, side - 1),
-        (half, side - 1),
+        (side - 1,),
+        (2 * side - 1,),
+        (half, 2, side - 1),
         (half, 2),
         (half, 2),
         (half, 2),
         (half, 2),
         (side, half),
-        (side, half),
+        (side, half, 2),
         (1,),
         (2,),
         (2,),
-        (2,),
-        (side, half),
-        (side, half),
+        (side,),
+        (side, 2),
+        (side, half, 2),
         (side,),
         (side,),
     ]
@@ -604,9 +691,19 @@
     return pl.pallas_call(
         functools.partial(kernel, side),
         out_shape=jax.ShapeDtypeStruct(tile, BF16),
-        in_specs=[pl.BlockSpec(memory_space=pltpu.VMEM)] * 9,
+        in_specs=[pl.BlockSpec(memory_space=pl.ANY)] * 9,
         out_specs=pl.BlockSpec(memory_space=pltpu.VMEM),
         scratch_shapes=[
+            pltpu.VMEM(tile, BF16),
+            pltpu.VMEM((8, 16), jnp.int32),
+            pltpu.VMEM((1, 256), jnp.int32),
+            pltpu.VMEM((1, 128), F32),
+            pltpu.VMEM(in_weight.shape, BF16),
+            pltpu.VMEM(gate_weight.shape, BF16),
+            pltpu.VMEM((1, 128), F32),
+            pltpu.VMEM(out_weight.shape, BF16),
+            pltpu.VMEM(bin_weight.shape[::-1], BF16),
+            pltpu.SemaphoreType.DMA((9,)),
             pltpu.VMEM(tile, BF16),
             pltpu.VMEM(tile, BF16),
             gathered,
@@ -618,12 +715,12 @@
             pltpu.VMEM((2, 64, 64), BF16),
             pltpu.VMEM((8, 16), F32),
             pltpu.VMEM((2, 8, 16), F32),
-            pltpu.VMEM((2, 128, 128), BF16),
-            pltpu.VMEM((256, 8, 128), F32),
+            gathered,
+            pltpu.VMEM((side, 2, 128, 128), BF16),
+            pltpu.VMEM((side, 2, 128, 128), F32),
             gathered,
             gathered,
-            gathered,
-            gathered,
+            pltpu.VMEM((2 * half, 16, 8, 128), F32),
             pltpu.VMEM((half, 2) + tile, BF16),
             pltpu.VMEM((half, 2) + tile, BF16),
             pltpu.VMEM((side,) + tile, BF16),
@@ -632,7 +729,7 @@
         ]
         + [pltpu.SemaphoreType.DMA(shape) for shape in sems],
         compiler_params=pltpu.CompilerParams(
-            collective_id=0, has_side_effects=True, vmem_limit_bytes=32 * 1024 * 1024
+            collective_id=0, has_side_effects=True, vmem_limit_bytes=60 * 1024 * 1024
         ),
     )(
         pair,
@@ -643,7 +740,7 @@
         gate_weight,
         hidden_gain[None, :],
         out_weight,
-        bin_weight,
+        bin_weight.T,
     )
 
 

time: 76.5 us -> 72.8 us (0.952)
  local copies, waits for them, and re-layouts: 3.92 us -> 1.38 us
  Pallas kernels: 72.2 us -> 71.2 us
    unnamed x18 -> x1, local copies, waits for them, and re-layouts: 3.92 us -> 1.38 us
    pallas_call x1, Pallas kernels: 72.2 us -> 71.2 us  [local(): pl.pallas_call(functools.partial(kernel, side), out_shape=jax.ShapeDtypeS...]
where the time goes in v2:
time: 72.8 us; the launch traced here: 72.6 us
  Pallas kernels  71.2 us (98%)
  local copies, waits for them, and re-layouts  1.38 us (2%)
    pallas_call x1, Pallas kernels, local(): pl.pallas_call(functools.partial(kernel, side), out_shape=jax.ShapeDtypeS...  71.2 us

profile of v2, /device:TPU:1, one launch (start us, length us, event | category | flops | bytes accessed | tf_op | source)
XLA Modules:
  0.0 72.6 jit_solution(8355393388650305965)
XLA Ops:
  0.0 71.2 %shard_map.91 = bf16[8,16,128]{2,1,0:T(8,128)(2,1)} custom-call(bf16[8,16,128]{2,1,0:T(8,128)(2,1)} %pair_hbm.1, s32[8,16]{1,0:T(8,128)} %labels_hbm.1, s32[1,256]{1,0:T(1,128)} %bitcast.5, f32[1,128]{1,0:T(1,128)} %bitcast.6, bf16[128,512]{1,0:T(8,128)(2,1)} %in_weight_hbm.1, bf16[128,128]{1,0:T(8,128)(2,1)} %gate_weight_hbm.1, f32[1,128]{1,0:T(1,128)} %bitcast.7, ...), custom_call_target="tpu_custom_call" | custom-call | tf_op jit(solution)/shard_map/pallas_call | solution.py:691
  71.2 1.4 %copy.11 = bf16[8,16,128]{2,1,0:T(8,128)(2,1)} copy(bf16[8,16,128]{2,1,0:T(8,128)(2,1)} %shard_map.91) | data formatting | bytes 65536

commit v3 on v2

--- a/solution.py
+++ b/solution.py
@@ -153,9 +153,9 @@
 
     operands = (
         (pair_hbm, pair_ref),
-        (norm_gain_hbm, norm_gain_ref),
         (in_weight_hbm, in_weight_ref),
         (mask_hbm, mask_ref),
+        (norm_gain_hbm, norm_gain_ref),
         (labels_hbm, labels_ref),
         (gate_weight_hbm, gate_weight_ref),
         (hidden_gain_hbm, hidden_gain_ref),
@@ -175,13 +175,12 @@
         else:
             pl.when(jnp.logical_not(is_self))(signal)
 
+    for index in range(9):
+        load(index).start()
+
     on_own_path = jnp.logical_and(
         jnp.logical_and(x == y, meet == x), jnp.logical_and(zh == zl, core == my_k_core)
     )
-    for there in range(side):
-        greet(
-            device(meet, x, there, zh, my_k_core), jnp.logical_and(on_own_path, there == zh)
-        )
     for slot in range(half):
         for there in range(2):
             source = core * half + slot
@@ -189,23 +188,24 @@
                 device(y, mine, zl, source, there),
                 jnp.logical_and(on_own_path, jnp.logical_and(source == zl, there == core)),
             )
-    for index in range(9):
-        load(index).start()
-    for step in range(1, 2 * side):
-        other = (zl * 2 + core + step) % (2 * side)
-        greet(device(x, y, zh, other // 2, other % 2))
+    for slot in range(half):
+        for there in range(2):
+            source = core * half + slot
+            greet(
+                device(x, y, zh, source, there),
+                jnp.logical_and(source == zl, there == core),
+            )
+    greet(device(x, y, zh, zl, 1 - core))
     for step in range(1, side):
         greet(device(x, (y + step) % side, zh, zl, core))
         greet(device((x + step) % side, y, zh, zl, core))
         greet(device((x + step) % side, y, zh, zl, 1 - core))
-    greetings = 2 * side - 1 + 3 * (side - 1) + 2 * side
-    awaited = greetings - 2 * on_own_path.astype(jnp.int32)
-
-    for index in range(5):
-        load(index).wait()
-    pair_float = pair_ref[...].astype(F32).reshape(128, 128)
-    normed_in, inverse_in, scaled_in = norm_parts(pair_float, norm_gain_ref[...])
-    inputs = scaled_in.astype(BF16)
+    greetings = 2 * side + 1 + 3 * (side - 1)
+    awaited = (
+        greetings - on_own_path.astype(jnp.int32) - (core == my_k_core).astype(jnp.int32)
+    )
+
+    load(2).wait()
     place = lax.broadcasted_iota(jnp.int32, (128, 256), 0)
     lane = lax.broadcasted_iota(jnp.int32, (128, 256), 1)
     mask_float = mask_ref[...].astype(F32)
@@ -218,14 +218,21 @@
         jnp.where(lane == first_col + place % 16, mask_float, 0.0), axis=1, keepdims=True
     )
     pair_mask = mask_i * mask_j
-    projected = jnp.dot(inputs, in_weight_ref[...], preferred_element_type=F32)
-    sig_a = jax.nn.sigmoid(projected[:, 0:128])
-    value_a = projected[:, 128:256]
-    sig_b = jax.nn.sigmoid(projected[:, 256:384])
-    value_b = projected[:, 384:512]
+    load(0).wait()
+    load(3).wait()
+    pair_float = pair_ref[...].astype(F32).reshape(128, 128)
+    normed_in, inverse_in, scaled_in = norm_parts(pair_float, norm_gain_ref[...])
+    inputs = scaled_in.astype(BF16)
+    load(1).wait()
+
+    def projected(first):
+        both = jnp.dot(
+            inputs, in_weight_ref[:, first : first + 256], preferred_element_type=F32
+        )
+        return jax.nn.sigmoid(both[:, 0:128]), both[:, 128:256]
+
+    sig_b, value_b = projected(256)
     right_own[...] = (sig_b * value_b * pair_mask).astype(BF16).reshape(8, 16, 128)
-    left_own[...] = (sig_a * value_a * pair_mask).astype(BF16).reshape(8, 16, 128)
-    label_out[...] = labels_ref[...].astype(F32)
     pl.semaphore_wait(barrier, awaited)
 
     def first_right(there):
@@ -258,20 +265,41 @@
             jnp.logical_and(diagonal, there == core),
         )
 
-    my_turn = my_k_slot * 2 + core
-    for phase in range(side):
-        push(*first_right((my_turn + phase) % side))
-    for there in range(side):
-        push(*first_left(there))
-
+    near = zh == 0
+    push(*first_right(0))
+
+    @pl.when(near)
+    def _():
+        for there in range(1, side):
+            push(*first_right(there))
+
+    sig_a, value_a = projected(0)
+    left_own[...] = (sig_a * value_a * pair_mask).astype(BF16).reshape(8, 16, 128)
+    push(*first_left(0))
+
+    @pl.when(near)
+    def _():
+        for there in range(1, side):
+            push(*first_left(there))
+
+    @pl.when(jnp.logical_not(near))
+    def _():
+        drain(*first_left(0))
+        for there in range(1, side):
+            push(*first_left(there))
+            push(*first_right(there))
+        drain(*first_right(0))
+
+    load(4).wait()
+    label_out[...] = labels_ref[...].astype(F32)
     for index in range(5, 9):
         load(index).wait()
 
     saved[0] = normed_in
-    saved[1] = sig_a
-    saved[2] = value_a
-    saved[3] = sig_b
-    saved[4] = value_b
+    saved[1] = value_a * pair_mask * sig_a * (1.0 - sig_a)
+    saved[2] = sig_a * pair_mask
+    saved[3] = value_b * pair_mask * sig_b * (1.0 - sig_b)
+    saved[4] = sig_b * pair_mask
     saved[5] = jax.nn.sigmoid(jnp.dot(inputs, gate_weight_ref[...], preferred_element_type=F32))
     saved[6] = jnp.broadcast_to(pair_mask, (128, 128))
     saved[7] = jnp.broadcast_to(inverse_in, (128, 128))
@@ -286,8 +314,7 @@
         )
 
     def turn_of(phase):
-        index = (zh - phase + side) % side
-        return index // 2, index % 2
+        return phase // 2, phase % 2
 
     def second_right(slot, part, step):
         return send(
@@ -362,9 +389,6 @@
         for step in range(1, side):
             who = (mine + step) % side
             arrived(right_all.at[who, slot, part], r_right2.at[who, slot, part])
-        if phase == side - 1:
-            for there in range(2):
-                push(*labels_to(there))
         tri_blocks(1 - core, slot, part)
         if phase == side - 1:
             fold(1 - core)
@@ -372,6 +396,8 @@
         tri_blocks(core, slot, part)
     fold(core)
     arrived(tri_in, r_tri.at[0])
+    for there in range(2):
+        push(*labels_to(there))
     triangle = tri_part[core] + tri_in[...]
 
     hidden_gain = hidden_gain_ref[...]
@@ -560,7 +586,7 @@
 
         def right_block(index, carry, step=step, who=who):
             slot = index // 2
-            part = index % 2
+            part = 1 - index % 2
             if step == 0:
                 sums = nothing
             else:
@@ -605,24 +631,24 @@
             value = term if value is None else value + term
         return value.reshape(128, 128)
 
-    grad_left = total_of(gl_own, r_gl2)
-    sig_a = saved[1]
-    value_a = saved[2]
-    masked = grad_left * mask_wide
-    proj_0 = (masked * value_a * sig_a * (1.0 - sig_a)).astype(BF16)
-    proj_1 = (masked * sig_a).astype(BF16)
-    grad_right = total_of(gr_own, r_gr2)
-    sig_b = saved[3]
-    value_b = saved[4]
-    masked = grad_right * mask_wide
-    proj_2 = (masked * value_b * sig_b * (1.0 - sig_b)).astype(BF16)
-    proj_3 = (masked * sig_b).astype(BF16)
-    grad_proj = jnp.concatenate([proj_0, proj_1, proj_2, proj_3], axis=-1)
-    grad_inputs = dot_nt(grad_proj, in_weight_ref[...]) + saved[9]
+    def project(grad, first):
+        grad_proj = jnp.concatenate(
+            [(grad * saved[first]).astype(BF16), (grad * saved[first + 1]).astype(BF16)], axis=-1
+        )
+        columns = (first - 1) * 128
+        return dot_nt(grad_proj, in_weight_ref[:, columns : columns + 256])
+
+    grad_inputs = saved[9] + project(total_of(gl_own, r_gl2), 1)
+    grad_inputs = grad_inputs + project(total_of(gr_own, r_gr2), 3)
     result = saved[8] + norm_back(grad_inputs, saved[0], saved[7], norm_gain_ref[...])
     out_ref[...] = result.astype(BF16).reshape(8, 16, 128)
 
-    for there in range(side):
+    @pl.when(near)
+    def _():
+        drain(*first_right(0))
+        drain(*first_left(0))
+
+    for there in range(1, side):
         drain(*first_right(there))
         drain(*first_left(there))
     for there in range(2):

time: 72.8 us -> 71 us (0.975)
  Pallas kernels: 71.2 us -> 69.2 us
    pallas_call x1, Pallas kernels: 71.2 us -> 69.2 us  [local(): pl.pallas_call(functools.partial(kernel, side), out_shape=jax.ShapeDtypeS...]
where the time goes in v3:
time: 71 us; the launch traced here: 70.6 us
  Pallas kernels  69.2 us (97%)
  local copies, waits for them, and re-layouts  1.38 us (2%)
    pallas_call x1, Pallas kernels, local(): pl.pallas_call(functools.partial(kernel, side), out_shape=jax.ShapeDtypeS...  69.2 us

profile of v3, /device:TPU:1, one launch (start us, length us, event | category | flops | bytes accessed | tf_op | source)
XLA Modules:
  0.0 70.6 jit_solution(3392698822463907648)
XLA Ops:
  0.0 69.2 %shard_map.91 = bf16[8,16,128]{2,1,0:T(8,128)(2,1)} custom-call(bf16[8,16,128]{2,1,0:T(8,128)(2,1)} %pair_hbm.1, s32[8,16]{1,0:T(8,128)} %labels_hbm.1, s32[1,256]{1,0:T(1,128)} %bitcast.5, f32[1,128]{1,0:T(1,128)} %bitcast.6, bf16[128,512]{1,0:T(8,128)(2,1)} %in_weight_hbm.1, bf16[128,128]{1,0:T(8,128)(2,1)} %gate_weight_hbm.1, f32[1,128]{1,0:T(1,128)} %bitcast.7, ...), custom_call_target="tpu_custom_call" | custom-call | tf_op jit(solution)/shard_map/pallas_call | solution.py:717
  69.2 1.4 %copy.11 = bf16[8,16,128]{2,1,0:T(8,128)(2,1)} copy(bf16[8,16,128]{2,1,0:T(8,128)(2,1)} %shard_map.91) | data formatting | bytes 65536

commit v4 on v3

--- a/solution.py
+++ b/solution.py
@@ -316,12 +316,12 @@
     def turn_of(phase):
         return phase // 2, phase % 2
 
-    def second_right(slot, part, step):
+    def second_right(slot, step):
         return send(
-            right_all.at[mine, slot, part],
-            right_all.at[mine, slot, part],
-            s_right2.at[slot, part, step - 1],
-            r_right2.at[mine, slot, part],
+            right_all.at[mine, slot],
+            right_all.at[mine, slot],
+            s_right2.at[slot, step - 1],
+            r_right2.at[mine, slot],
             device((x + step) % side, y, zh, zl, core),
         )
 
@@ -331,11 +331,11 @@
         for step in range(1, side):
             second_left(slot, step).start()
 
-    def forward(phase):
-        slot, part = turn_of(phase)
-        arrived(right_all.at[mine, slot, part], r_right1.at[slot, part])
+    def forward(slot):
+        for part in range(2):
+            arrived(right_all.at[mine, slot, part], r_right1.at[slot, part])
         for step in range(1, side):
-            second_right(slot, part, step).start()
+            second_right(slot, step).start()
 
     acc[...] = jnp.zeros_like(acc)
 
@@ -378,8 +378,8 @@
 
     forward(0)
     for phase in range(side):
-        if phase < side - 1:
-            forward(phase + 1)
+        if phase % 2 == 0 and phase // 2 + 1 < half:
+            forward(phase // 2 + 1)
         slot, part = turn_of(phase)
         if phase == 0:
             for step in range(1, side):
@@ -388,7 +388,8 @@
                     arrived(left_all.at[who, there], r_left2.at[who, there])
         for step in range(1, side):
             who = (mine + step) % side
-            arrived(right_all.at[who, slot, part], r_right2.at[who, slot, part])
+            if part == 0:
+                arrived(right_all.at[who, slot], r_right2.at[who, slot])
         tri_blocks(1 - core, slot, part)
         if phase == side - 1:
             fold(1 - core)
@@ -586,7 +587,7 @@
 
         def right_block(index, carry, step=step, who=who):
             slot = index // 2
-            part = 1 - index % 2
+            part = index % 2
             if step == 0:
                 sums = nothing
             else:
@@ -662,9 +663,9 @@
     for slot in range(half):
         for step in range(1, side):
             second_left(slot, step).wait_send()
+            second_right(slot, step).wait_send()
         for there in range(2):
             for step in range(1, side):
-                second_right(slot, there, step).wait_send()
                 third_left(slot, there, step).wait_send()
             drain(*fourth_left(slot, there))
             drain(*fourth_right(slot, there))
@@ -688,7 +689,7 @@
         (side,),
         (side,),
         (half, side - 1),
-        (half, 2, side - 1),
+        (half, side - 1),
         (1,),
         (2,),
         (2,),
@@ -700,7 +701,7 @@
         (half, 2),
         (half, 2),
         (side, half),
-        (side, half, 2),
+        (side, half),
         (1,),
         (2,),
         (2,),

time: 71 us -> 67.6 us (0.952)
  Pallas kernels: 69.2 us -> 65.9 us
    pallas_call x1, Pallas kernels: 69.2 us -> 65.9 us  [local(): pl.pallas_call(functools.partial(kernel, side), out_shape=jax.ShapeDtypeS...]
where the time goes in v4:
time: 67.6 us; the launch traced here: 67.3 us
  Pallas kernels  65.9 us (97%)
  local copies, waits for them, and re-layouts  1.38 us (2%)
    pallas_call x1, Pallas kernels, local(): pl.pallas_call(functools.partial(kernel, side), out_shape=jax.ShapeDtypeS...  65.9 us
    unnamed x1, local copies, waits for them, and re-layouts  1.38 us

profile of v4, /device:TPU:1, one launch (start us, length us, event | category | flops | bytes accessed | tf_op | source)
XLA Modules:
  0.0 67.3 jit_solution(1429906962496103565)
XLA Ops:
  0.0 65.9 %shard_map.91 = bf16[8,16,128]{2,1,0:T(8,128)(2,1)} custom-call(bf16[8,16,128]{2,1,0:T(8,128)(2,1)} %pair_hbm.1, s32[8,16]{1,0:T(8,128)} %labels_hbm.1, s32[1,256]{1,0:T(1,128)} %bitcast.5, f32[1,128]{1,0:T(1,128)} %bitcast.6, bf16[128,512]{1,0:T(8,128)(2,1)} %in_weight_hbm.1, bf16[128,128]{1,0:T(8,128)(2,1)} %gate_weight_hbm.1, f32[1,128]{1,0:T(1,128)} %bitcast.7, ...), custom_call_target="tpu_custom_call" | custom-call | tf_op jit(solution)/shard_map/pallas_call | solution.py:718
  65.9 1.4 %copy.11 = bf16[8,16,128]{2,1,0:T(8,128)(2,1)} copy(bf16[8,16,128]{2,1,0:T(8,128)(2,1)} %shard_map.91) | data formatting | bytes 65536

commit v5 on v4

--- a/solution.py
+++ b/solution.py
@@ -175,9 +175,6 @@
         else:
             pl.when(jnp.logical_not(is_self))(signal)
 
-    for index in range(9):
-        load(index).start()
-
     on_own_path = jnp.logical_and(
         jnp.logical_and(x == y, meet == x), jnp.logical_and(zh == zl, core == my_k_core)
     )
@@ -188,6 +185,8 @@
                 device(y, mine, zl, source, there),
                 jnp.logical_and(on_own_path, jnp.logical_and(source == zl, there == core)),
             )
+    for index in range(9):
+        load(index).start()
     for slot in range(half):
         for there in range(2):
             source = core * half + slot
@@ -266,12 +265,13 @@
         )
 
     near = zh == 0
-    push(*first_right(0))
 
     @pl.when(near)
     def _():
-        for there in range(1, side):
+        for there in sorted(range(1, side), key=lambda there: abs(there - half)):
             push(*first_right(there))
+
+    push(*first_right(0))
 
     sig_a, value_a = projected(0)
     left_own[...] = (sig_a * value_a * pair_mask).astype(BF16).reshape(8, 16, 128)

time: 67.6 us -> 67.7 us (level)
  no operation moved by 1% of the time
where the time goes in v5:
time: 67.7 us; the launch traced here: 67 us
  Pallas kernels  65.6 us (97%)
  local copies, waits for them, and re-layouts  1.38 us (2%)
    pallas_call x1, Pallas kernels, local(): pl.pallas_call(functools.partial(kernel, side), out_shape=jax.ShapeDtypeS...  65.6 us
    unnamed x1, local copies, waits for them, and re-layouts  1.38 us

profile of v5, /device:TPU:1, one launch (start us, length us, event | category | flops | bytes accessed | tf_op | source)
XLA Modules:
  0.0 67.0 jit_solution(5821014342893737246)
XLA Ops:
  0.0 65.6 %shard_map.91 = bf16[8,16,128]{2,1,0:T(8,128)(2,1)} custom-call(bf16[8,16,128]{2,1,0:T(8,128)(2,1)} %pair_hbm.1, s32[8,16]{1,0:T(8,128)} %labels_hbm.1, s32[1,256]{1,0:T(1,128)} %bitcast.5, f32[1,128]{1,0:T(1,128)} %bitcast.6, bf16[128,512]{1,0:T(8,128)(2,1)} %in_weight_hbm.1, bf16[128,128]{1,0:T(8,128)(2,1)} %gate_weight_hbm.1, f32[1,128]{1,0:T(1,128)} %bitcast.7, ...), custom_call_target="tpu_custom_call" | custom-call | tf_op jit(solution)/shard_map/pallas_call | solution.py:718
  65.6 1.4 %copy.11 = bf16[8,16,128]{2,1,0:T(8,128)(2,1)} copy(bf16[8,16,128]{2,1,0:T(8,128)(2,1)} %shard_map.91) | data formatting | bytes 65536
